TPU v7x, 512 devices: a whole 4x4x16 slice. The times are simulated.
512 devices in a mesh: tower: 4 (over x), wide: 128 (over z, y, core).
Axes of the slice: x: 4, y: 4, z: 16, core: 2. Of those that a mesh axis runs over, the one named last changes fastest.
Arguments:
- user_rows: bfloat16 [196608, 512], P('wide', 'tower'), may hold values from -6 to 6
- positive_rows: bfloat16 [196608, 512], P('wide', 'tower'), may hold values from -6 to 6
- centroids: float32 [4096, 512], P('wide'), may hold values from -3.5 to 3.5
- residuals: bfloat16 [4096, 256, 512], P('wide', 'tower'), may hold values from -6 to 6
- block_lists: int32 [1024, 16], P('wide'), may hold values from 0 to 4095, as said below
- block_lengths: int32 [1024], P('wide'), may hold values from 1 to 16, 8192 in all
- cluster_counts: int32 [4096], P('wide'), may hold values from 64 to 4096
- ad_counts: int32 [4096, 256], P('wide'), may hold values from 1 to 256
Outputs:
- user_loss: float32 [196608], P('wide')
- user_grad: float32 [196608, 512], P('wide', 'tower')
- centroid_grad: float32 [4096, 512], P('wide', 'tower')
Inputs may be any that keep to these rules, and one draw needn't show every extreme that they name: `block_lists`: on one index of wide, the 128 list entries name different clusters; at most 1 of them lie on one shard (cluster id // 32), and on some shard exactly 1. Entries at or past a block's length are ignored.
All inputs are finite; a program needn't handle non-finite values. No bound on the sum of `block_lengths` on one device may be relied on, other than what follows from the above.
Results may differ from a plain program's by a relative error of at most 0.0035.
Values may be sent and summed in bfloat16 or wider, within the bound.
A program may use at most 128 MiB of HBM per device.

v0:
```python
import math

import jax
import jax.numpy as jnp
from jax import lax
from jax.sharding import PartitionSpec as P

LOSS_SCALE = 16


def slot_plan(flat_ids, shards, capacity, per_shard):
    source = flat_ids // per_shard
    local_ids = flat_ids % per_shard
    position = jnp.arange(flat_ids.shape[0])
    before = (source[None, :] == source[:, None]) & (position[None, :] < position[:, None])
    ranking = jnp.sum(before.astype(jnp.int32), axis=1)
    slot_ids = source * capacity + ranking
    wanted = jnp.full((shards * capacity,), -1, jnp.int32).at[slot_ids].set(local_ids)
    return (slot_ids, wanted)


def local(
    user_rows,
    positive_rows,
    centroids,
    residuals,
    block_lists,
    block_lengths,
    cluster_counts,
    ad_counts,
):
    shards = lax.axis_size("wide")
    tower_index = lax.axis_index("tower")
    per_shard, width = centroids.shape
    quarter = residuals.shape[1]
    blocks, listed = block_lists.shape
    entries = blocks * listed
    capacity = (entries + shards - 1) // shards
    rows_block = user_rows.shape[0] // blocks
    score_scale = 1.0 / math.sqrt(width)
    ad_rows = (centroids[:, None, :] + residuals.astype(jnp.float32)).astype(jnp.bfloat16)
    ad_weights = ad_counts.astype(jnp.float32)
    expected = (
        cluster_counts.astype(jnp.float32)[:, None]
        * ad_weights
        / jnp.sum(ad_weights, axis=1, keepdims=True)
    )
    correction = lax.dynamic_slice_in_dim(
        jnp.log(expected), tower_index * quarter, quarter, 1
    ).astype(jnp.bfloat16)
    slot_ids, wanted = slot_plan(block_lists.reshape(entries), shards, capacity, per_shard)
    incoming = lax.all_to_all(
        wanted.reshape(shards, capacity), "wide", split_axis=0, concat_axis=0, tiled=True
    )
    chosen = jnp.maximum(incoming, 0)
    sent_tiles = ad_rows[chosen]
    sent_shift = correction[chosen]
    came_tiles, came_shift = (
        lax.all_to_all(sent_tiles, "wide", split_axis=0, concat_axis=0, tiled=True),
        lax.all_to_all(sent_shift, "wide", split_axis=0, concat_axis=0, tiled=True),
    )
    tile_rows = came_tiles.reshape(shards * capacity, quarter, width)[slot_ids].reshape(
        blocks, listed * quarter, width
    )
    log_shift = (
        came_shift.reshape(shards * capacity, quarter)[slot_ids]
        .reshape(blocks, listed * quarter)
        .astype(jnp.float32)
    )
    full_users = lax.all_gather(user_rows, "tower", axis=1, tiled=True).reshape(
        blocks, rows_block, width
    )
    logits = (
        jnp.einsum("bue,bae->bua", full_users, tile_rows, preferred_element_type=jnp.float32)
        * score_scale
        - log_shift[:, None, :]
    )
    used_slots = (jnp.arange(listed * quarter) // quarter)[None, :] < block_lengths[:, None]
    logits = jnp.where(used_slots[:, None, :], logits, -jnp.inf)
    local_max = jnp.max(logits, axis=2)
    local_sum = jnp.sum(jnp.exp(logits - local_max[:, :, None]), axis=2)
    positive_wide = positive_rows.astype(jnp.float32)
    partial_dot = jnp.sum(user_rows.astype(jnp.float32) * positive_wide, axis=1).reshape(
        blocks, rows_block
    )
    global_max = lax.pmax(local_max, "tower")
    global_sum, positive_dot = lax.psum(
        (local_sum * jnp.exp(local_max - global_max), partial_dot), "tower"
    )
    positive_logit = positive_dot * score_scale
    ceiling = jnp.maximum(global_max, positive_logit)
    log_total = ceiling + jnp.log(
        global_sum * jnp.exp(global_max - ceiling) + jnp.exp(positive_logit - ceiling)
    )
    row_loss = (log_total - positive_logit).reshape(blocks * rows_block)
    softmax_probs = jnp.exp(logits - log_total[:, :, None]).astype(jnp.bfloat16)
    positive_prob = jnp.exp(positive_logit - log_total).reshape(blocks * rows_block)
    ad_term = jnp.einsum(
        "bua,bae->bue", softmax_probs, tile_rows, preferred_element_type=jnp.float32
    ).reshape(blocks * rows_block, width)
    summed_term = lax.psum_scatter(ad_term, "tower", scatter_dimension=1, tiled=True)
    user_grad = (
        LOSS_SCALE * score_scale * (summed_term + (positive_prob - 1.0)[:, None] * positive_wide)
    )
    quarter_mass = jnp.sum(
        softmax_probs.reshape(blocks, rows_block, listed, quarter), axis=3, dtype=jnp.float32
    ).astype(jnp.bfloat16)
    slot_grad = jnp.einsum(
        "buk,bue->bke", quarter_mass, full_users, preferred_element_type=jnp.float32
    ).reshape(entries, width)
    slot_table = (
        jnp.zeros((shards * capacity, width), jnp.float32)
        .at[slot_ids]
        .set(slot_grad)
        .reshape(shards, capacity, width)
    )
    owner_map = (incoming[:, :, None] == jnp.arange(per_shard)[None, None, :]).astype(jnp.float32)
    returned = lax.all_to_all(slot_table, "wide", split_axis=0, concat_axis=0, tiled=True)
    owned = jnp.einsum("dcl,dce->le", owner_map, returned, precision=lax.Precision.HIGHEST)
    section = lax.psum_scatter(owned, "tower", scatter_dimension=1, tiled=True)
    centroid_grad = LOSS_SCALE * score_scale * section
    return (row_loss, user_grad, centroid_grad)


def solution(mesh):
    return jax.shard_map(
        local,
        mesh=mesh,
        in_specs=(
            P("wide", "tower"),
            P("wide", "tower"),
            P("wide", None),
            P("wide", "tower", None),
            P("wide", None),
            P("wide"),
            P("wide"),
            P("wide", None),
        ),
        out_specs=(P("wide"), P("wide", "tower"), P("wide", "tower")),
        check_vma=False,
    )
```

profile of v0, /device:TPU:1, one launch (start us, length us, event | category | flops | bytes accessed | tf_op | source)
XLA Modules:
  0.0 624.2 jit_solution(11242127667641637732)
XLA Ops:
  7.2 0.8 reshape.283
  7.9 0.8 reshape.282
  8.7 0.2 convert_reduce_fusion
  8.9 0.0 copy-start.6
  8.9 1.0 scatter_custom_fusion
  9.9 0.7 copy.20
  10.6 20.6 %all-to-all-start = ((s32[128,1,1]{2,1,0:T(1,128)}), s32[128,1,1]{2,1,0:T(1,128)S(1)}, u32[]{:S(2)}, u32[]{:S(2)}) async-start(s32[128,1,1]{2,1,0:T(1,128)} %copy.20), calls=%async_computation | async-start | bytes 131072 | tf_op jit(solution)/shard_map/all_to_all | solution.py:52
  31.2 0.9 convert_reduce_fusion.1
  32.1 0.8 convert_element_type.44
  32.9 0.7 convert_element_type.43
  33.5 0.1 fusion.15
  33.6 12.4 %all-to-all-done = s32[128,1,1]{2,1,0:T(1,128)S(1)} async-done(((s32[128,1,1]{2,1,0:T(1,128)}), s32[128,1,1]{2,1,0:T(1,128)S(1)}, u32[]{:S(2)}, u32[]{:S(2)}) %all-to-all-start) | async-done | bytes 544 | tf_op jit(solution)/shard_map/all_to_all | solution.py:52
  46.0 5.1 fusion.27
  51.1 0.7 gather_fusion.2
  51.8 0.7 copy.21
  52.5 5.6 all-to-all-start.2
  58.2 2.1 add_convert_fusion
  60.3 6.6 %gather_fusion = bf16[128,64,512]{2,1,0:T(8,128)(2,1)} fusion(bf16[32,64,512]{2,1,0:T(8,128)(2,1)S(1)} %add_convert_fusion, s32[1024]{0:T(1024)S(1)} %pad_clamp_fusion.1), kind=kCustom, calls=%fused_computation | custom fusion | bytes 16777728 | tf_op jit(solution)/shard_map/gather | solution.py:56
  66.9 6.3 %all-to-all-done.2 = bf16[128,1,64]{2,1,0:T(2,128)(2,1)S(1)} async-done(((bf16[128,1,64]{2,1,0:T(2,128)(2,1)}), bf16[128,1,64]{2,1,0:T(2,128)(2,1)S(1)}, u32[]{:S(2)}, u32[]{:S(2)}) %all-to-all-start.2) | async-done | bytes 16416 | tf_op jit(solution)/shard_map/all_to_all | solution.py:60
  73.2 0.0 copy-start
  73.2 0.0 copy-start.1
  73.2 10.5 %all-to-all-start.1 = ((bf16[128,1,64,512]{3,2,1,0:T(8,128)(2,1)}), bf16[128,1,64,512]{3,2,1,0:T(8,128)(2,1)}, u32[]{:S(2)}, u32[]{:S(2)}) async-start(bf16[128,1,64,512]{3,2,1,0:T(8,128)(2,1)} %bitcast.48), calls=%async_computation.1 | async-start | bytes 16777216 | tf_op jit(solution)/shard_map/all_to_all | solution.py:59
  83.7 0.0 all-gather.2.cloned.1.call-start
  83.8 0.7 all-gather.2.cloned.1.call-update
  84.5 0.0 reduce-scatter.5.cloned.1.call-start
  84.5 0.0 copy-done
  84.5 0.0 copy-done.1
  84.6 0.3 fusion.4
  84.8 0.1 reshape.288
  84.9 0.0 copy-done.6
  84.9 0.0 copy-done.5
  84.9 0.1 broadcast_compare_fusion
  85.0 0.7 gather_fusion.3
  85.7 0.1 reshape.295
  85.8 362.8 %all-to-all-done.1 = bf16[128,1,64,512]{3,2,1,0:T(8,128)(2,1)} async-done(((bf16[128,1,64,512]{3,2,1,0:T(8,128)(2,1)}), bf16[128,1,64,512]{3,2,1,0:T(8,128)(2,1)}, u32[]{:S(2)}, u32[]{:S(2)}) %all-to-all-start.1) | async-done | bytes 8388640 | tf_op jit(solution)/shard_map/all_to_all | solution.py:59
  448.6 10.0 %gather_fusion.1 = bf16[128,64,512]{2,1,0:T(8,128)(2,1)} fusion(bf16[128,64,512]{2,1,0:T(8,128)(2,1)} %bitcast.4, s32[1024]{0:T(1024)S(1)} %pad_clamp_fusion), kind=kCustom, calls=%fused_computation.1 | custom fusion | bytes 16777728 | tf_op jit(solution)/shard_map/gather | solution.py:62
  458.6 9.4 %bitcast_reduce_fusion = (f32[8,192]{1,0:T(8,128)S(1)}, f32[8,1024,192]{1,2,0:T(8,128)}) fusion(f32[8,1024]{1,0:T(8,128)S(1)} %reshape.295, pred[8,1024]{1,0:T(8,128)(4,1)S(1)} %broadcast_compare_fusion, bf16[8,1024,512]{2,1,0:T(8,128)(2,1)} %bitcast.46, bf16[8,192,512]{2,1,0:T(8,128)(2,1)} %bitcast.51), kind=kOutput, calls=%fused_computation.8 | convolution fusion | flops 1616902656 | bytes 16300032 | tf_op jit(solution)/shard_map/bue,bae->bua/dot_general | solution.py:74
  468.0 8.6 %pmax.7 = f32[8,192]{1,0:T(8,128)S(1)} all-reduce(f32[8,192]{1,0:T(8,128)S(1)} %get-tuple-element.11), channel_id=1, replica_groups=mesh['tower'=4,'wide'=128] {'tower'}, use_global_device_ids=true, to_apply=%region_4.5 | all-reduce | flops 1536 | bytes 12288 | tf_op jit(solution)/shard_map/pmax | solution.py:86
  476.5 0.0 copy-done.2
  476.5 3.8 fusion.1
  480.3 10.8 %all-reduce = (f32[8,192]{1,0:T(8,128)S(1)}, f32[8,192]{1,0:T(8,128)S(1)}) all-reduce(f32[8,192]{1,0:T(8,128)S(1)} %exponential_multiply_fusion, f32[8,192]{1,0:T(8,128)S(1)} %reshape.288), channel_id=1, replica_groups=mesh['tower'=4,'wide'=128] {'tower'}, use_global_device_ids=true, to_apply=%region_8.9 | all-reduce | flops 3072 | bytes 24576 | tf_op jit(solution)/shard_map/psum | solution.py:87
  491.2 0.6 exponential_add_fusion
  491.8 0.0 copy-done.3
  491.8 3.7 fusion.3
  495.5 0.0 copy-start.4
  495.5 4.1 copy.24
  499.6 3.6 bitcast_reduce_fusion.1
  503.3 2.4 fusion.29
  505.7 2.1 scatter_custom_fusion.1
  507.8 1.1 reshape.293
  508.9 37.3 %all_to_all.27 = f32[128,1,512]{2,1,0:T(1,128)S(1)} all-to-all(f32[128,1,512]{2,1,0:T(1,128)S(1)} %reshape.293), channel_id=1, replica_groups=mesh['tower'=4,'wide'=128] {'wide'}, dimensions={0} | all-to-all | bytes 524288 | tf_op jit(solution)/shard_map/all_to_all | solution.py:118
  546.2 0.0 copy-done.4
  546.2 0.8 fusion.7
  547.1 0.0 reduce-scatter.5.cloned.1.call-update
  547.1 0.0 reduce-scatter.3.cloned.1.call-start
  547.2 6.9 %fusion.28 = f32[8,192,512]{2,1,0:T(8,128)} fusion(bf16[8,192,1024]{2,1,0:T(8,128)(2,1)S(1)} %fusion.3, bf16[8,1024,512]{2,1,0:T(8,128)(2,1)} %bitcast.47), kind=kOutput, calls=%fused_computation.72 | convolution fusion | flops 1610612736 | bytes 14680064 | tf_op jit(solution)/shard_map/bua,bae->bue/dot_general | solution.py:98
  554.1 0.0 reduce-scatter.3.cloned.1.call-update
  554.1 0.8 sub.75
  554.9 0.7 multiply_subtract_fusion
  555.6 0.7 reshape.289
  556.3 8.0 %reduce-scatter.5.cloned.1.call-done = f32[32,128]{1,0:T(8,128)} async-done(((f32[32,512]{1,0:T(8,128)}), f32[32,128]{1,0:T(8,128)}) %reduce-scatter.5.cloned.1.call-update) | async-done | bytes 16400 | tf_op jit(solution)/shard_map/reduce_scatter | solution.py:120
  564.3 1.3 broadcast_multiply_fusion
  565.6 49.8 %reduce-scatter.3.cloned.1.call-done = f32[1536,128]{1,0:T(8,128)} async-done(((f32[1536,512]{1,0:T(8,128)}), f32[1536,128]{1,0:T(8,128)}) %reduce-scatter.3.cloned.1.call-update) | async-done | bytes 786448 | tf_op jit(solution)/shard_map/reduce_scatter | solution.py:101
  615.4 2.3 fusion.6
  (11 shorter events, 0.1 us)
Async XLA Ops:
  8.9 76.0 %copy-start.6 = (s32[128]{0:T(128)}, s32[128]{0:T(128)S(1)}, u32[]{:S(2)}) copy-start(s32[128]{0:T(128)S(1)} %fusion.24) | copy-start | bytes 1540
  10.6 35.4 %all-to-all-start = ((s32[128,1,1]{2,1,0:T(1,128)}), s32[128,1,1]{2,1,0:T(1,128)S(1)}, u32[]{:S(2)}, u32[]{:S(2)}) async-start(s32[128,1,1]{2,1,0:T(1,128)} %copy.20), calls=%async_computation | async-start | bytes 131072 | tf_op jit(solution)/shard_map/all_to_all | solution.py:52
  52.5 20.7 %all-to-all-start.2 = ((bf16[128,1,64]{2,1,0:T(2,128)(2,1)}), bf16[128,1,64]{2,1,0:T(2,128)(2,1)S(1)}, u32[]{:S(2)}, u32[]{:S(2)}) async-start(bf16[128,1,64]{2,1,0:T(2,128)(2,1)} %copy.21), calls=%async_computation.2 | async-start | bytes 131072 | tf_op jit(solution)/shard_map/all_to_all | solution.py:60
  73.2 11.3 %copy-start = (bf16[1536,128]{1,0:T(8,128)(2,1)S(1)}, bf16[1536,128]{1,0:T(8,128)(2,1)}, u32[]{:S(2)}) copy-start(bf16[1536,128]{1,0:T(8,128)(2,1)} %param.8) | copy-start | bytes 1179652
  73.2 11.3 %copy-start.1 = (bf16[1536,128]{1,0:T(8,128)(2,1)S(1)}, bf16[1536,128]{1,0:T(8,128)(2,1)}, u32[]{:S(2)}) copy-start(bf16[1536,128]{1,0:T(8,128)(2,1)} %param.9) | copy-start | bytes 1179652
  73.2 11.7 %copy-start.5 = (s32[8]{0:T(128)S(1)}, s32[8]{0:T(128)}, u32[]{:S(2)}) copy-start(s32[8]{0:T(128)} %param.13) | copy-start | bytes 100
  73.2 375.4 %all-to-all-start.1 = ((bf16[128,1,64,512]{3,2,1,0:T(8,128)(2,1)}), bf16[128,1,64,512]{3,2,1,0:T(8,128)(2,1)}, u32[]{:S(2)}, u32[]{:S(2)}) async-start(bf16[128,1,64,512]{3,2,1,0:T(8,128)(2,1)} %bitcast.48), calls=%async_computation.1 | async-start | bytes 16777216 | tf_op jit(solution)/shard_map/all_to_all | solution.py:59
  83.7 374.8 %all-gather.2.cloned.1.call-start = ((), (), s32[]{:S(2)}) async-start(), calls=%async_computation.6 | async-start | bytes 1966080 | tf_op jit(solution)/shard_map/all_gather | solution.py:70
  84.5 479.8 %reduce-scatter.5.cloned.1.call-start = ((), (), s32[]{:S(2)}) async-start(), calls=%async_computation.8 | async-start | bytes 81920 | tf_op jit(solution)/shard_map/reduce_scatter | solution.py:120
  85.8 390.7 %copy-start.2 = (f32[8,1024]{1,0:T(8,128)}, f32[8,1024]{1,0:T(8,128)S(1)}, u32[]{:S(2)}) copy-start(f32[8,1024]{1,0:T(8,128)S(1)} %reshape.295) | copy-start | bytes 98308
  491.2 0.6 copy-start.3
  495.5 50.8 %copy-start.4 = (s32[128]{0:T(128)S(1)}, s32[128]{0:T(128)}, u32[]{:S(2)}) copy-start(s32[128]{0:T(128)} %get-tuple-element.3) | copy-start | bytes 1540
  547.1 68.3 %reduce-scatter.3.cloned.1.call-start = ((), (), s32[]{:S(2)}) async-start(), calls=%async_computation.7 | async-start | bytes 3932160 | tf_op jit(solution)/shard_map/reduce_scatter | solution.py:101
Sparse Core Ops, SparseCore 0:
  86.7 37.7 all-gather.1
  547.2 16.9 reduce-scatter.4
  567.4 48.0 reduce-scatter.2
where the time goes:
time: 625 us; the launch traced here: 624 us
  waiting for transfers between devices  440 us (70%)
  blocking collectives  56.7 us (9%)
  starting transfers between devices  36.8 us (6%)
  local copies, waits for them, and re-layouts  30.9 us (5%)
  other arithmetic  26.2 us (4%)
  matrix products  19.6 us (3%)
  between operations  13.9 us (2%)
    all_to_all x1, waiting for transfers between devices, local(): lax.all_to_all(sent_tiles, 'wide', split_axis=0, concat_axis=0, tiled=True)  363 us
    reduce_scatter x1, waiting for transfers between devices, local(): lax.psum_scatter(ad_term, 'tower', scatter_dimension=1, tiled=True)  49.8 us
    all_to_all x1, blocking collectives, local(): lax.all_to_all(slot_table, 'wide', split_axis=0, concat_axis=0, tiled=True)  37.3 us
    all_to_all x1, starting transfers between devices, local(): lax.all_to_all(wanted.reshape(shards, capacity), 'wide', split_axis=0, co...  20.6 us
  transfers between devices with their start and end apart: 6, of which 5 were waited for; matrix products, arithmetic and copies ran while one was open for 5% of the time, Pallas kernels for 0%

commit v1 on v0

v1 whole, which is shorter than its diff:
```python
import functools
import math

import jax
import jax.numpy as jnp
from jax import lax
from jax.experimental import pallas as pl
from jax.experimental.pallas import tpu as pltpu
from jax.sharding import Mesh, PartitionSpec as P

LOSS_SCALE = 16
AXES = ("x", "z", "y", "c")
SPLIT = (16, 4, 2)
LOW = -1e30
MESH = pl.DeviceIdType.MESH
HBM = pl.BlockSpec(memory_space=pl.ANY)
VMEM = pl.BlockSpec(memory_space=pltpu.VMEM)
SMEM = pl.BlockSpec(memory_space=pltpu.SMEM)
CODE_ROWS = 16


def remote(src, dst, sends, recvs, k, where):
    return pltpu.make_async_remote_copy(
        src_ref=src,
        dst_ref=dst,
        send_sem=sends.at[k],
        recv_sem=recvs.at[k],
        device_id=where,
        device_id_type=MESH,
    )


def greet(peers):
    barrier = pltpu.get_barrier_semaphore()
    for where in peers:
        pl.semaphore_signal(barrier, inc=1, device_id=where, device_id_type=MESH)
    pl.semaphore_wait(barrier, len(peers))


def gather_kernel(
    sizes, tiles, users, positives, codes, shift,
    all_tiles, all_users, own_positives, all_shift, sends, recvs, locals_,
):
    nx, nz, ny, nc = sizes
    x, z, y, c = (lax.axis_index(a) for a in AXES)
    rows = users.shape[0] // nx
    depth = users.shape[1]
    half = tiles.shape[1]
    quarter = half // 2
    at_x = lambda d: lax.rem(x + d + nx, nx)
    at_y = lambda d: lax.rem(y + d + ny, ny)
    at_z = lambda d: lax.rem(z + d + nz, nz)
    to_x = lambda d: {"x": at_x(d)}
    to_y = lambda d: {"y": at_y(d)}
    to_z = lambda d: {"z": at_z(d)}
    sibling = {"c": 1 - c}

    greet(
        [to_x(d) for d in range(1, nx)]
        + [to_y(d) for d in range(1, ny)]
        + [to_z(1), to_z(-1), sibling]
    )

    count = [0]
    sent = []

    def push(src, dst, where, landing):
        k = count[0]
        count[0] += 1
        copy = remote(src, dst, sends, recvs, k, where)
        copy.start()
        sent.append(copy)
        return remote(landing, landing, sends, recvs, k, where)

    columns = lambda i: pl.ds(pl.multiple_of(i * depth, depth), depth)
    part = lambda i: pl.ds(pl.multiple_of(i * rows, rows), rows)
    home = all_users.at[z, c]

    def block(h, a, b):
        return all_tiles.at[at_y(b), at_x(a), h] if h == 0 else all_tiles.at[at_y(a), at_x(b), h]

    first = (to_x, to_y)
    second = (to_y, to_x)
    lower, upper = pl.ds(0, quarter), pl.ds(quarter, quarter)

    arrivals = []
    for d in range(1, nx):
        arrivals.append(
            push(
                users.at[part(at_x(d))], home.at[pl.ds(0, rows), columns(x)], to_x(d),
                home.at[pl.ds(0, rows), columns(at_x(-d))],
            )
        )
    p1 = {}
    for h in (0, 1):
        for d in (1, -1):
            p1[h, d] = push(tiles.at[h], block(h, 0, 0), first[h](d), block(h, -d, 0))
    own = [
        pltpu.make_async_copy(users.at[part(x)], home.at[pl.ds(0, rows), columns(x)], locals_.at[0]),
        pltpu.make_async_copy(codes, home.at[pl.ds(rows, CODE_ROWS)], locals_.at[1]),
        pltpu.make_async_copy(tiles, all_tiles.at[y, x], locals_.at[2]),
        pltpu.make_async_copy(shift, all_shift.at[y], locals_.at[3]),
        pltpu.make_async_copy(positives.at[part(x)], own_positives.at[:, columns(x)], locals_.at[4]),
    ]
    for copy in own:
        copy.start()
    late = []
    p2 = {}
    for h in (0, 1):
        for d in (1, -1):
            p2[h, 0, d] = push(tiles.at[h], block(h, 0, 0), second[h](d), block(h, 0, -d))
    for d in range(1, nx):
        late.append(
            push(
                positives.at[part(at_x(d))], own_positives.at[:, columns(x)], to_x(d),
                own_positives.at[:, columns(at_x(-d))],
            )
        )
    for d in range(1, ny):
        late.append(push(shift, all_shift.at[y], to_y(d), all_shift.at[at_y(-d)]))

    for arrival in arrivals:
        arrival.wait_recv()
    own[0].wait()
    own[1].wait()

    chunk = lambda d: all_users.at[at_z(d), c]
    other = lambda d: all_users.at[at_z(d), 1 - c]
    steps = nz // 2
    up, down = {}, {}

    def ring(s):
        if s > 0:
            up[s - 1].wait_recv()
            if s - 1 in down:
                down[s - 1].wait_recv()
        if s < steps:
            up[s] = push(chunk(-s), chunk(-s), to_z(1), chunk(-s - 1))
        if s < steps - 1:
            down[s] = push(chunk(s), chunk(s), to_z(-1), chunk(s + 1))
        late.append(push(chunk(-s), chunk(-s), sibling, other(-s)))
        if 0 < s < steps:
            late.append(push(chunk(s), chunk(s), sibling, other(s)))

    turns = list(range(steps + 1))
    ring(turns.pop(0))
    while len(turns) > steps - 3 and turns:
        ring(turns.pop(0))

    for h in (0, 1):
        for d in (1, -1):
            p1[h, d].wait_recv()
    q = {}
    for h in (0, 1):
        for d in (1, -1):
            cut = lower if d == 1 else upper
            q[h, d] = push(
                block(h, -d, 0).at[cut], block(h, -d, 0).at[cut], first[h](d), block(h, -2 * d, 0).at[cut]
            )
    for j in (1, -1):
        for h in (0, 1):
            for d in (1, -1):
                p2[h, j, d] = push(block(h, j, 0), block(h, j, 0), second[h](d), block(h, j, -d))
    if turns:
        ring(turns.pop(0))

    def onward(j):
        for h in (0, 1):
            for d in (1, -1):
                p2[h, j, d].wait_recv()
                cut = lower if d == 1 else upper
                late.append(
                    push(
                        block(h, j, -d).at[cut], block(h, j, -d).at[cut], second[h](d),
                        block(h, j, -2 * d).at[cut],
                    )
                )

    onward(0)
    for h in (0, 1):
        for d in (1, -1):
            q[h, d].wait_recv()
    for h in (0, 1):
        for d in (1, -1):
            p2[h, 2, d] = push(block(h, 2, 0), block(h, 2, 0), second[h](d), block(h, 2, -d))
    if turns:
        ring(turns.pop(0))
    onward(1)
    while turns:
        ring(turns.pop(0))
    onward(-1)
    onward(2)
    for arrival in late:
        arrival.wait_recv()
    for copy in own[2:]:
        copy.wait()
    for copy in sent:
        copy.wait_send()
    assert count[0] == sends.shape[0], count[0]


def fetch(users, tiles, list_ref, ubuf, tbuf, usem, tsem, half, e, slot):
    b, tile = list_ref[0, e], list_ref[1, e]
    per = 2 * half
    yp, cl = tile // per, tile % per
    w, i = b // 2, b % 2
    rows = ubuf.shape[1]
    return (
        pltpu.make_async_copy(
            users.at[w, pl.ds(pl.multiple_of(i * rows, rows), rows)], ubuf.at[slot], usem.at[slot]
        ),
        pltpu.make_async_copy(
            tiles.at[yp, :, cl // half, cl % half], tbuf.at[slot], tsem.at[slot]
        ),
    )


def scores(ubuf, tbuf, shift_ref, slot, tile, scale):
    user = ubuf[slot]
    ads = tbuf[slot].reshape(tbuf.shape[1] * tbuf.shape[2], tbuf.shape[3])
    pick = lax.broadcasted_iota(jnp.int32, (shift_ref.shape[0], user.shape[0]), 0) == tile
    shift = lax.dot_general(
        shift_ref[...], pick.astype(jnp.float32).astype(jnp.bfloat16), (((0,), (0,)), ((), ())),
        preferred_element_type=jnp.float32,
    )
    raw = lax.dot_general(ads, user, (((1,), (1,)), ((), ())), preferred_element_type=jnp.float32)
    return user, ads, raw * scale - shift


def stats_kernel(
    half, scale, codes, mine, users, tiles, shift_ref,
    stats, list_ref, zeroed, ubuf, tbuf, zbuf, usem, tsem, zsem,
):
    nw = users.shape[0]
    ny = tiles.shape[0]
    rows = ubuf.shape[1]
    t = mine[0]
    zbuf[...] = jnp.zeros_like(zbuf)
    piece = zbuf.shape[0]
    zeros = [
        pltpu.make_async_copy(zbuf, zeroed.at[pl.ds(k * piece, piece)], zsem.at[k])
        for k in range(zeroed.shape[0] // piece)
    ]
    for copy in zeros:
        copy.start()

    def gather(w, n):
        for i in range(2):
            for yp in range(ny):
                list_ref[0, n] = w * 2 + i
                list_ref[1, n] = yp * (2 * half) + codes[1, w * ny + yp]
                n = n + (codes[0, w * ny + yp] == 2 * t + i).astype(jnp.int32)
        return n

    total = lax.fori_loop(0, nw, gather, jnp.int32(0))
    list_ref[0, total] = -1
    list_ref[1, total] = 0
    list_ref[2, 0] = total
    stats[:, 0:1, :] = jnp.full((stats.shape[0], 1, stats.shape[2]), LOW, jnp.float32)
    stats[:, 1:2, :] = jnp.zeros((stats.shape[0], 1, stats.shape[2]), jnp.float32)
    get = functools.partial(fetch, users, tiles, list_ref, ubuf, tbuf, usem, tsem, half)

    @pl.when(total > 0)
    def _():
        for copy in get(0, 0):
            copy.start()

    def step(e, _):
        slot = e % 2

        @pl.when(e + 1 < total)
        def _():
            for copy in get(e + 1, 1 - slot):
                copy.start()

        for copy in get(e, slot):
            copy.wait()
        b, tile = list_ref[0, e], list_ref[1, e]
        _, _, logits = scores(ubuf, tbuf, shift_ref, slot, tile, scale)
        before = stats[b, 0:1, 0:rows]
        held = stats[b, 1:2, 0:rows]
        top = jnp.maximum(before, jnp.max(logits, axis=0, keepdims=True))
        stats[b, 0:1, 0:rows] = top
        stats[b, 1:2, 0:rows] = held * jnp.exp(before - top) + jnp.sum(
            jnp.exp(logits - top), axis=0, keepdims=True
        )
        return 0

    lax.fori_loop(0, total, step, 0)
    for copy in zeros:
        copy.wait()


def as_row(column):
    n = column.shape[0]
    eye = lax.broadcasted_iota(jnp.int32, (n, n), 0) == lax.broadcasted_iota(jnp.int32, (n, n), 1)
    return jnp.sum(jnp.where(eye, column, 0.0), axis=0, keepdims=True)


def as_column(row):
    n = row.shape[1]
    eye = lax.broadcasted_iota(jnp.int32, (n, n), 0) == lax.broadcasted_iota(jnp.int32, (n, n), 1)
    return jnp.sum(jnp.where(eye, row, 0.0), axis=1, keepdims=True)


def total_kernel(
    sizes, scale, stats, user, positive, totals, losses, factor,
    came, mine, got, lost, s1, r1, s2, r2, s3, r3,
):
    nx, nz, ny, nc = sizes
    x, z, y, c = (lax.axis_index(a) for a in AXES)
    nw = nz * nc
    me = z * nc + c
    rows = user.shape[0] // 2
    barrier = pltpu.get_barrier_semaphore()

    def there(d):
        p = lax.rem(me + d, nw)
        return p, {"z": p // nc, "c": p % nc}

    def hello(d, _):
        pl.semaphore_signal(barrier, inc=1, device_id=there(d)[1], device_id_type=MESH)
        return 0

    lax.fori_loop(1, nw, hello, 0)
    for d in range(1, nx):
        pl.semaphore_signal(
            barrier, inc=1, device_id={"x": lax.rem(x + d, nx)}, device_id_type=MESH
        )
    pl.semaphore_wait(barrier, nw - 1 + nx - 1)

    def out(d, _):
        p, where = there(d)
        remote(stats.at[p], came.at[me], s1, r1, d, where).start()
        return 0

    lax.fori_loop(1, nw, out, 0)
    dots = []
    for i in range(2):
        u = user[i * rows:(i + 1) * rows].astype(jnp.float32)
        v = positive[i * rows:(i + 1) * rows].astype(jnp.float32)
        dots.append(as_row(jnp.sum(u * v, axis=1, keepdims=True)) * scale)

    def landed(d, _):
        p, where = there(nw - d)
        remote(came.at[p], came.at[p], s1, r1, d, where).wait_recv()
        return 0

    lax.fori_loop(1, nw, landed, 0)
    came[pl.ds(me, 1)] = stats[pl.ds(me, 1)]
    mine[...] = jnp.zeros_like(mine)
    factor[...] = jnp.zeros_like(factor)
    lost[pl.ds(x, 1)] = jnp.zeros((1,) + lost.shape[1:], jnp.float32)
    for i in range(2):
        tops = came[:, i, 0:1, 0:rows]
        sums = came[:, i, 1:2, 0:rows]
        ceiling = jnp.maximum(jnp.max(tops, axis=0), dots[i])
        whole = jnp.sum(sums * jnp.exp(tops - ceiling[None]), axis=0) + jnp.exp(dots[i] - ceiling)
        log_total = ceiling + jnp.log(whole)
        mine[i, :, 0:rows] = log_total
        lost[pl.ds(x, 1), i, :, 0:rows] = (log_total - dots[i])[None]
        factor[i, :, 0:rows] = jnp.exp(dots[i] - log_total) - 1.0

    def back(d, _):
        _, where = there(d)
        remote(mine, got.at[me], s2, r2, d, where).start()
        return 0

    lax.fori_loop(1, nw, back, 0)
    for d in range(1, nx):
        remote(lost.at[x], lost.at[x], s3, r3, d, {"x": lax.rem(x + d, nx)}).start()
    got[pl.ds(me, 1)] = mine[...][None]

    def done(d, _):
        p, where = there(nw - d)
        remote(got.at[p], got.at[p], s2, r2, d, where).wait_recv()
        return 0

    lax.fori_loop(1, nw, done, 0)
    totals[...] = got[...]
    for d in range(1, nx):
        frm = lax.rem(x - d + nx, nx)
        remote(lost.at[frm], lost.at[frm], s3, r3, d, {"x": frm}).wait_recv()
    losses[...] = lost[...]

    def left(d, _):
        p, where = there(d)
        remote(stats.at[p], came.at[me], s1, r1, d, where).wait_send()
        remote(mine, got.at[me], s2, r2, d, where).wait_send()
        return 0

    lax.fori_loop(1, nw, left, 0)
    for d in range(1, nx):
        remote(lost.at[x], lost.at[x], s3, r3, d, {"x": lax.rem(x + d, nx)}).wait_send()


def grads_kernel(
    half, scale, list_ref, users, tiles, shift_ref, totals, _zeroed,
    grads, cluster, ubuf, tbuf, acc, gout, usem, tsem, gsem,
):
    rows = ubuf.shape[1]
    parts = tbuf.shape[1]
    total = list_ref[2, 0]
    cluster[...] = jnp.zeros_like(cluster)
    get = functools.partial(fetch, users, tiles, list_ref, ubuf, tbuf, usem, tsem, half)

    @pl.when(total > 0)
    def _():
        for copy in get(0, 0):
            copy.start()

    def put(b, slot):
        return pltpu.make_async_copy(gout.at[slot], grads.at[b], gsem.at[slot])

    def step(e, n):
        slot = e % 2

        @pl.when(e + 1 < total)
        def _():
            for copy in get(e + 1, 1 - slot):
                copy.start()

        for copy in get(e, slot):
            copy.wait()
        b, tile = list_ref[0, e], list_ref[1, e]
        fresh = jnp.logical_or(e == 0, list_ref[0, jnp.maximum(e - 1, 0)] != b)
        last = list_ref[0, e + 1] != b
        user, ads, logits = scores(ubuf, tbuf, shift_ref, slot, tile, scale)
        probs = jnp.exp(logits - totals[b, :, 0:rows]).astype(jnp.bfloat16)
        wide = probs.astype(jnp.float32).reshape(parts, probs.shape[0] // parts, rows)
        mass = jnp.sum(wide, axis=1).astype(jnp.bfloat16)
        slots = jnp.dot(mass, user, preferred_element_type=jnp.float32)
        cluster[pl.ds(tile, 1)] += jnp.sum(slots, axis=0, keepdims=True)[None]
        term = lax.dot_general(probs, ads, (((0,), (0,)), ((), ())), preferred_element_type=jnp.float32)

        @pl.when(fresh)
        def _():
            acc[...] = term

        @pl.when(jnp.logical_not(fresh))
        def _():
            acc[...] += term

        @pl.when(last)
        def _():
            to = n % 2

            @pl.when(n >= 2)
            def _():
                put(0, to).wait()

            gout[to] = acc[...].astype(jnp.bfloat16)
            put(b, to).start()

        return n + last.astype(jnp.int32)

    n = lax.fori_loop(0, total, step, jnp.int32(0))
    for k in range(2):
        @pl.when(n > k)
        def _():
            put(0, k).wait()


def return_kernel(
    sizes, factor_scale, grads, cluster, factor, positive, user_grad, centroid_grad,
    own, sib, up_out, up_in, down_out, down_in, final, landed, parts,
    own_sem, sib_s, sib_r, up_s, up_r, down_s, down_r, fin_s, fin_r, cl_s, cl_r,
):
    nx, nz, ny, nc = sizes
    x, z, y, c = (lax.axis_index(a) for a in AXES)
    at_z = lambda d: lax.rem(z + d + nz, nz)
    above, below = {"z": at_z(1)}, {"z": at_z(-1)}
    sibling = {"c": 1 - c}
    rows, width = own.shape[2], own.shape[3]
    depth = width // nx
    steps = nz // 2
    pairs = [(dx, dy) for dx in range(nx) for dy in range(ny) if dx or dy]
    place = lambda dx, dy: (lax.rem(x + dx + nx, nx), lax.rem(y + dy + ny, ny))
    greet(
        [dict(zip(("x", "y"), place(dx, dy))) for dx, dy in pairs] + [above, below, sibling]
    )
    order = []
    for s in range(steps):
        order.append(steps - s)
        if s < steps - 1:
            order.append(s + 1 - steps)
    order.append(0)
    loads, crossing = {}, {}
    for k, d in enumerate(order):
        loads[d] = pltpu.make_async_copy(grads.at[at_z(d), c], own.at[k], own_sem.at[k])
        loads[d].start()
        crossing[d] = remote(grads.at[at_z(d), 1 - c], sib.at[k], sib_s, sib_r, k, sibling)
        crossing[d].start()
    columns = lambda i: pl.ds(pl.multiple_of(i * depth, depth), depth)
    clusters = []
    for k, (dx, dy) in enumerate(pairs):
        px, py = place(dx, dy)
        copy = remote(
            cluster.at[py, px], parts.at[k], cl_s, cl_r, k, {"x": px, "y": py}
        )
        copy.start()
        clusters.append(copy)
    index = {d: k for k, d in enumerate(order)}

    def both(d, i):
        return own[index[d], i].astype(jnp.float32) + sib[index[d], i].astype(jnp.float32)

    def ready(d):
        loads[d].wait()
        crossing[d].wait_recv()

    ups = lambda s, i: remote(up_out.at[s, i], up_in.at[s, i], up_s, up_r, 2 * s + i, above)
    downs = lambda s, i: remote(down_out.at[s, i], down_in.at[s, i], down_s, down_r, 2 * s + i, below)
    for s in range(steps):
        ready(steps - s)
        if s < steps - 1:
            ready(s + 1 - steps)
        for i in range(2):
            value = both(steps - s, i)
            if s > 0:
                ups(s - 1, i).wait_recv()
                value = value + up_in[s - 1, i].astype(jnp.float32)
            up_out[s, i] = value.astype(jnp.bfloat16)
            ups(s, i).start()
            if s < steps - 1:
                value = both(s + 1 - steps, i)
                if s > 0:
                    downs(s - 1, i).wait_recv()
                    value = value + down_in[s - 1, i].astype(jnp.float32)
                down_out[s, i] = value.astype(jnp.bfloat16)
                downs(s, i).start()
    ready(0)
    for i in range(2):
        downs(steps - 2, i).wait_recv()
        ups(steps - 1, i).wait_recv()
        value = (
            both(0, i)
            + up_in[steps - 1, i].astype(jnp.float32)
            + down_in[steps - 2, i].astype(jnp.float32)
        )
        wide = positive[i * rows:(i + 1) * rows].astype(jnp.float32)
        value = (value + as_column(factor[i, :, 0:rows]) * wide) * factor_scale
        for k in range(nx):
            final[k, i * rows:(i + 1) * rows] = value[:, k * depth:(k + 1) * depth]
    ends = []
    for d in range(1, nx):
        px = lax.rem(x + d, nx)
        copy = remote(final.at[px], landed.at[x], fin_s, fin_r, d, {"x": px})
        copy.start()
        ends.append(copy)
    whole = cluster[y, x]
    for k in range(len(pairs)):
        clusters[k].wait_recv()
        whole = whole + parts[k]
    centroid_grad[...] = whole * factor_scale
    user_grad[pl.ds(x, 1)] = final[pl.ds(x, 1)]
    for d in range(1, nx):
        frm = lax.rem(x - d + nx, nx)
        remote(landed.at[frm], landed.at[frm], fin_s, fin_r, d, {"x": frm}).wait_recv()
        user_grad[pl.ds(frm, 1)] = landed[pl.ds(frm, 1)]
    for copy in list(crossing.values()) + clusters + ends:
        copy.wait_send()
    for i in range(2):
        for s in range(steps):
            ups(s, i).wait_send()
        for s in range(steps - 1):
            downs(s, i).wait_send()


def params(identity=None, megabytes=48):
    return pltpu.CompilerParams(
        collective_id=identity,
        has_side_effects=identity is not None,
        vmem_limit_bytes=megabytes * 1024 * 1024,
    )


def local(
    sizes, user_rows, positive_rows, centroids, residuals, block_lists, block_lengths,
    cluster_counts, ad_counts,
):
    nx, nz, ny, nc = sizes
    x, z, y, c = (lax.axis_index(a) for a in AXES)
    nw, shards = nz * nc, nz * ny * nc
    per, width = centroids.shape
    quarter = residuals.shape[1]
    tile = ad_counts.shape[1]
    blocks, listed = block_lists.shape
    rows = user_rows.shape[0] // blocks
    half = per // 2
    scale = 1.0 / math.sqrt(width)
    sds = jax.ShapeDtypeStruct
    dma = pltpu.SemaphoreType.DMA
    bf16, f32 = jnp.bfloat16, jnp.float32

    ad_rows = (centroids[:, None, :] + residuals.astype(f32)).astype(bf16)
    weights = ad_counts.astype(f32)
    expected = (
        cluster_counts.astype(f32)[:, None] * weights / jnp.sum(weights, axis=1, keepdims=True)
    )
    shift = jnp.log(expected).astype(bf16)
    flat = block_lists.reshape(blocks * listed)
    used = jnp.arange(listed)[None, :] < block_lengths[:, None]
    name = jnp.where(used, jnp.arange(blocks)[:, None] + 1, 0).reshape(blocks * listed)
    match = flat[:, None] // per == jnp.arange(shards)[None, :]
    block_of = jnp.sum(jnp.where(match, name[:, None], 0), axis=0) - 1
    place_of = jnp.sum(jnp.where(match, (flat % per)[:, None], 0), axis=0)
    codes = jnp.stack([block_of, place_of]).astype(f32).astype(bf16)
    codes = jnp.pad(codes, ((0, CODE_ROWS - 2), (0, width - shards)))

    steps = nz // 2
    copies = 2 * (nx - 1) + (ny - 1) + 8 + 4 + 12 + 16 + (nz - 1) + nz
    mine = 2 * rows
    all_tiles, all_users, positives, all_shift = pl.pallas_call(
        functools.partial(gather_kernel, sizes),
        out_shape=(
            sds((ny, nx, 2, half, quarter, width), bf16),
            sds((nz, nc, mine + CODE_ROWS, width), bf16),
            sds((mine, width), bf16),
            sds((ny, per, tile), bf16),
        ),
        in_specs=[HBM] * 5,
        out_specs=[HBM] * 4,
        scratch_shapes=[dma((copies,)), dma((copies,)), dma((5,))],
        compiler_params=params(0, 4),
        name="gather",
    )(ad_rows.reshape(2, half, quarter, width), user_rows, positive_rows, codes, shift)

    picked = all_users[:, :, mine:mine + 2, :shards].reshape(nw, 2, nz, ny, nc)
    picked = lax.dynamic_index_in_dim(picked, z, 2, keepdims=False)
    picked = lax.dynamic_index_in_dim(picked, c, 3, keepdims=False)
    places = jnp.swapaxes(picked, 0, 1).reshape(2, nw * ny).astype(jnp.int32)
    flat_users = all_users.reshape(nw, mine + CODE_ROWS, width)
    flat_shift = all_shift.reshape(ny * per, tile)
    lanes = -(-rows // 128) * 128
    buffers = [pltpu.VMEM((2, rows, width), bf16), pltpu.VMEM((2, nx, quarter, width), bf16)]
    stats, entries, zeroed = pl.pallas_call(
        functools.partial(stats_kernel, half, scale),
        out_shape=(
            sds((2 * nw, 2, lanes), f32),
            sds((3, nw * ny + 8), jnp.int32),
            sds((2 * nw, rows, width), bf16),
        ),
        in_specs=[SMEM, SMEM, HBM, HBM, VMEM],
        out_specs=[VMEM, SMEM, HBM],
        scratch_shapes=buffers
        + [pltpu.VMEM((4, rows, width), bf16), dma((2,)), dma((2,)), dma((nw // 2,))],
        compiler_params=params(),
        name="stats",
    )(places, x.astype(jnp.int32).reshape(1), flat_users, all_tiles, flat_shift)

    own_users = lax.dynamic_index_in_dim(flat_users, z * nc + c, 0, keepdims=False)[:mine]
    totals, losses, factor = pl.pallas_call(
        functools.partial(total_kernel, sizes, scale),
        out_shape=(
            sds((nw, 2, 1, lanes), f32),
            sds((nx, 2, 1, lanes), f32),
            sds((2, 1, lanes), f32),
        ),
        in_specs=[VMEM] * 3,
        out_specs=[VMEM] * 3,
        scratch_shapes=[
            pltpu.VMEM((nw, 2, 2, lanes), f32),
            pltpu.VMEM((2, 1, lanes), f32),
            pltpu.VMEM((nw, 2, 1, lanes), f32),
            pltpu.VMEM((nx, 2, 1, lanes), f32),
        ]
        + [dma((nw,))] * 4
        + [dma((nx,))] * 2,
        compiler_params=params(1, 24),
        name="totals",
    )(stats.reshape(nw, 2, 2, lanes), own_users, positives)

    grads, cluster = pl.pallas_call(
        functools.partial(grads_kernel, half, scale),
        out_shape=(sds((2 * nw, rows, width), bf16), sds((ny * per, 1, width), f32)),
        in_specs=[SMEM, HBM, HBM, VMEM, VMEM, HBM],
        out_specs=[HBM, VMEM],
        input_output_aliases={5: 0},
        scratch_shapes=buffers
        + [
            pltpu.VMEM((rows, width), f32), pltpu.VMEM((2, rows, width), bf16),
            dma((2,)), dma((2,)), dma((2,)),
        ],
        compiler_params=params(),
        name="grads",
    )(entries, flat_users, all_tiles, flat_shift, totals.reshape(2 * nw, 1, lanes), zeroed)

    depth = width // nx
    cluster = jnp.swapaxes(cluster.reshape(ny, per, nx, depth), 1, 2)
    ring = lambda n: pltpu.VMEM((n, 2, rows, width), bf16)
    user_grad, centroid_grad = pl.pallas_call(
        functools.partial(return_kernel, sizes, LOSS_SCALE * scale),
        out_shape=(sds((nx, mine, depth), f32), sds((per, depth), f32)),
        in_specs=[HBM, VMEM, VMEM, VMEM],
        out_specs=[VMEM, VMEM],
        scratch_shapes=[
            ring(nz), ring(nz), ring(steps), ring(steps), ring(steps - 1), ring(steps - 1),
            pltpu.VMEM((nx, mine, depth), f32),
            pltpu.VMEM((nx, mine, depth), f32),
            pltpu.VMEM((nx * ny - 1, per, depth), f32),
            dma((nz,)), dma((nz,)), dma((nz,)),
            dma((2 * steps,)), dma((2 * steps,)), dma((2 * steps,)), dma((2 * steps,)),
            dma((nx,)), dma((nx,)), dma((nx * ny,)), dma((nx * ny,)),
        ],
        compiler_params=params(2, 48),
        name="return",
    )(grads.reshape(nz, nc, 2, rows, width), cluster, factor, positives)
    return (
        losses[:, :, 0, :rows].reshape(blocks * rows),
        user_grad.reshape(blocks * rows, depth),
        centroid_grad,
    )


def build(mesh, sizes):
    return jax.shard_map(
        functools.partial(local, sizes),
        mesh=mesh,
        in_specs=(
            P(("z", "y", "c"), "x"),
            P(("z", "y", "c"), "x"),
            P(("z", "y", "c"), None),
            P(("z", "y", "c"), "x", None),
            P(("z", "y", "c"), None),
            P(("z", "y", "c")),
            P(("z", "y", "c")),
            P(("z", "y", "c"), None),
        ),
        out_specs=(P(("z", "y", "c")), P(("z", "y", "c"), "x"), P(("z", "y", "c"), "x")),
        check_vma=False,
    )


def solution(mesh):
    sizes = (mesh.shape["tower"],) + SPLIT
    return build(Mesh(mesh.devices.reshape(sizes), AXES), sizes)
```

time: 625 us -> 382 us (0.61)
  waiting for transfers between devices: 440 us -> 0 us
  Pallas kernels: 0 us -> 352 us
  blocking collectives: 56.7 us -> 0 us
  starting transfers between devices: 36.8 us -> 0 us
  other arithmetic: 26.2 us -> 5.51 us
  matrix products: 19.6 us -> 0 us
  between operations: 13.9 us -> 0.81 us
  local copies, waits for them, and re-layouts: 30.9 us -> 21.4 us
    all_to_all x3 -> x0, waiting for transfers between devices: 382 us -> none  [the longest x1 363 us: local(): lax.all_to_all(sent_tiles, 'wide', split_axis=0, concat_axis=0, tiled=True)]
    pallas_call x0 -> x5, Pallas kernels: none -> 352 us  [the longest x1 192 us: local(): pl.pallas_call(functools.partial(gather_kernel, sizes), out_shape=(sds((n...]
    reduce_scatter x2 -> x0, waiting for transfers between devices: 57.8 us -> none  [the longest x1 49.8 us: local(): lax.psum_scatter(ad_term, 'tower', scatter_dimension=1, tiled=True)]
    all_to_all x1 -> x0, blocking collectives: 37.3 us -> none  [local(): lax.all_to_all(slot_table, 'wide', split_axis=0, concat_axis=0, tiled=True)]
    all_to_all x3 -> x0, starting transfers between devices: 36.7 us -> none  [the longest x1 20.6 us: local(): lax.all_to_all(wanted.reshape(shards, capacity), 'wide', split_axis=0, co...]
    dot_general x4 -> x0, matrix products: 19.6 us -> none  [the longest x1 9.4 us: local(): jnp.einsum('bue,bae->bua', full_users, tile_rows, preferred_element_type=...]
    gather x5 -> x0, local copies, waits for them, and re-layouts: 18.6 us -> none  [the longest x1 9.96 us: local(): came_tiles.reshape(shards * capacity, quarter, width)[slot_ids]]
    unnamed x14 -> x11, local copies, waits for them, and re-layouts: 0.03 us -> 17.3 us
  transfers between devices with their start and end apart: 6 -> 0, of which waited for: 5 -> 0; matrix products, arithmetic and copies ran while one was open for 5% -> 0% of each run, Pallas kernels for 0% -> 0%
where the time goes in v1:
time: 382 us; the launch traced here: 380 us
  Pallas kernels  352 us (92%)
  local copies, waits for them, and re-layouts  21.4 us (6%)
  other arithmetic  5.51 us (1%)
    pallas_call x1, Pallas kernels, local(): pl.pallas_call(functools.partial(gather_kernel, sizes), out_shape=(sds((n...  192 us
    pallas_call x1, Pallas kernels, local(): pl.pallas_call(functools.partial(return_kernel, sizes, LOSS_SCALE * scale...  88.6 us
    pallas_call x1, Pallas kernels, local(): pl.pallas_call(functools.partial(total_kernel, sizes, scale), out_shape=(...  39.2 us
    unnamed x11, local copies, waits for them, and re-layouts  17.3 us
    pallas_call x1, Pallas kernels, local(): pl.pallas_call(functools.partial(grads_kernel, half, scale), out_shape=(s...  16.2 us
    pallas_call x1, Pallas kernels, local(): pl.pallas_call(functools.partial(stats_kernel, half, scale), out_shape=(s...  16 us

profile of v1, /device:TPU:1, one launch (start us, length us, event | category | flops | bytes accessed | tf_op | source)
XLA Modules:
  0.0 379.7 jit_solution(13935991235439558947)
XLA Ops:
  0.6 0.0 copy-start.3
  0.6 0.0 copy-start.2
  0.7 0.8 broadcast_in_dim_reshape.4
  1.5 0.7 convert_element_type.36
  2.2 0.9 convert_reduce_fusion
  3.0 0.7 fusion
  3.8 0.1 select_n.57
  3.9 0.1 select_reduce_fusion.1
  4.0 0.8 log_convert_fusion.shift
  4.9 2.1 add_convert_fusion
  7.0 0.0 copy-done.3
  7.0 0.0 copy-done.2
  7.0 192.0 %gather.1 = (bf16[4,4,2,16,64,512]{5,4,3,2,1,0:T(8,128)(2,1)S(1)}, bf16[16,2,400,512]{3,2,1,0:T(8,128)(2,1)S(1)}, bf16[384,512]{1,0:T(8,128)(2,1)S(1)}, bf16[4,32,256]{2,1,0:T(8,128)(2,1)S(1)}) custom-call(bf16[2,16,64,512]{3,2,1,0:T(8,128)(2,1)S(1)} %bitcast.23, bf16[1536,128]{1,0:T(8,128)(2,1)S(1)} %copy-done.2, bf16[1536,128]{1,0:T(8,128)(2,1)S(1)} %copy-done.3, ...), custom_call_target="tpu_custom_call" | custom-call | tf_op jit(solution)/shard_map/gather/pallas_call | solution.py:614
  199.0 0.0 copy-start
  199.0 11.1 %copy-done = bf16[4,4,2,16,64,512]{5,4,3,2,1,0:T(8,128)(2,1)} copy-done((bf16[4,4,2,16,64,512]{5,4,3,2,1,0:T(8,128)(2,1)}, bf16[4,4,2,16,64,512]{5,4,3,2,1,0:T(8,128)(2,1)S(1)}, u32[]{:S(2)}) %copy-start) | copy-done | bytes 33554456
  210.1 0.0 copy-start.1
  210.1 4.6 %copy-done.1 = bf16[16,2,400,512]{3,2,1,0:T(8,128)(2,1)} copy-done((bf16[16,2,400,512]{3,2,1,0:T(8,128)(2,1)}, bf16[16,2,400,512]{3,2,1,0:T(8,128)(2,1)S(1)}, u32[]{:S(2)}) %copy-start.1) | copy-done | bytes 13107224
  214.7 2.2 reshape.178
  217.0 0.1 dynamic-slice_convert_fusion
  217.1 0.1 copy.21
  217.2 0.1 copy.17
  217.3 0.1 reshape.176.codes
  217.4 16.0 %stats.1 = (f32[64,2,256]{2,1,0:T(2,128)S(1)}, s32[3,136]{1,0:T(4,128)S(1)}, bf16[64,192,512]{2,1,0:T(8,128)(2,1)}) custom-call(s32[2,128]{1,0:T(2,128)S(1)} %reshape.176.codes, s32[1]{0:T(128)} %bitcast.5.mine, bf16[32,400,512]{2,1,0:T(8,128)(2,1)} %bitcast.21, bf16[4,4,2,16,64,512]{5,4,3,2,1,0:T(8,128)(2,1)} %copy-done, bf16[128,256]{1,0:T(8,128)(2,1)S(1)} %bitcast.27), custom_call_target="tpu_custom_call" | custom-call | tf_op jit(solution)/shard_map/stats/pallas_call | solution.py:637
  233.4 39.2 %totals.1 = (f32[32,2,1,256]{3,2,1,0:T(1,128)S(1)}, f32[4,2,1,256]{3,2,1,0:T(1,128)S(1)}, f32[2,1,256]{2,1,0:T(1,128)S(1)}) custom-call(f32[32,2,2,256]{3,2,1,0:T(2,128)S(1)} %bitcast.29, bf16[384,512]{1,0:T(8,128)(2,1)S(1)} %dynamic-slice_bitcast_fusion.user, bf16[384,512]{1,0:T(8,128)(2,1)S(1)} %get-tuple-element.21.positive), custom_call_target="tpu_custom_call" | custom-call | tf_op jit(solution)/shard_map/totals/pallas_call | solution.py:653
  272.7 0.7 reshape_squeeze.3
  273.3 16.2 %grads.1 = (bf16[64,192,512]{2,1,0:T(8,128)(2,1)}, f32[128,1,512]{2,1,0:T(1,128)S(1)}) custom-call(s32[3,136]{1,0:T(4,128)S(1)} %get-tuple-element.23.list_ref, bf16[32,400,512]{2,1,0:T(8,128)(2,1)} %bitcast.22, bf16[4,4,2,16,64,512]{5,4,3,2,1,0:T(8,128)(2,1)} %copy-done, bf16[128,256]{1,0:T(8,128)(2,1)S(1)} %bitcast.28, ...), custom_call_target="tpu_custom_call", output_to_operand_aliasing={{0}: (5, {})} | custom-call | tf_op jit(solution)/shard_map/grads/pallas_call | solution.py:674
  289.6 88.6 %return.1 = (f32[4,384,128]{2,1,0:T(8,128)S(1)}, f32[32,128]{1,0:T(8,128)S(1)}) custom-call(bf16[16,2,2,192,512]{4,3,2,1,0:T(8,128)(2,1)} %bitcast.31, f32[4,4,32,128]{3,2,1,0:T(8,128)S(1)} %bitcast.24, f32[2,1,256]{2,1,0:T(1,128)S(1)} %get-tuple-element.28.factor, bf16[384,512]{1,0:T(8,128)(2,1)S(1)} %get-tuple-element.21.positive), custom_call_target="tpu_custom_call" | custom-call | tf_op jit(solution)/shard_map/return/pallas_call | solution.py:692
  378.2 0.9 copy.27
  379.1 0.6 copy.28
  (9 shorter events, 0.1 us)
Async XLA Ops:
  0.6 6.4 %copy-start.3 = (bf16[1536,128]{1,0:T(8,128)(2,1)S(1)}, bf16[1536,128]{1,0:T(8,128)(2,1)}, u32[]{:S(2)}) copy-start(bf16[1536,128]{1,0:T(8,128)(2,1)} %positives.1) | copy-start | bytes 1179652
  0.6 6.4 %copy-start.2 = (bf16[1536,128]{1,0:T(8,128)(2,1)S(1)}, bf16[1536,128]{1,0:T(8,128)(2,1)}, u32[]{:S(2)}) copy-start(bf16[1536,128]{1,0:T(8,128)(2,1)} %users.1) | copy-start | bytes 1179652
  199.0 11.1 %copy-start = (bf16[4,4,2,16,64,512]{5,4,3,2,1,0:T(8,128)(2,1)}, bf16[4,4,2,16,64,512]{5,4,3,2,1,0:T(8,128)(2,1)S(1)}, u32[]{:S(2)}) copy-start(bf16[4,4,2,16,64,512]{5,4,3,2,1,0:T(8,128)(2,1)S(1)} %get-tuple-element.18.tiles) | copy-start | bytes 100663296
  210.1 4.6 %copy-start.1 = (bf16[16,2,400,512]{3,2,1,0:T(8,128)(2,1)}, bf16[16,2,400,512]{3,2,1,0:T(8,128)(2,1)S(1)}, u32[]{:S(2)}) copy-start(bf16[16,2,400,512]{3,2,1,0:T(8,128)(2,1)S(1)} %get-tuple-element.17) | copy-start | bytes 39321604

commit v2 on v1

--- a/solution.py
+++ b/solution.py
@@ -17,6 +17,7 @@
 VMEM = pl.BlockSpec(memory_space=pltpu.VMEM)
 SMEM = pl.BlockSpec(memory_space=pltpu.SMEM)
 CODE_ROWS = 16
+SLOTS = 8
 
 
 def remote(src, dst, sends, recvs, k, where):
@@ -39,7 +40,7 @@
 
 def gather_kernel(
     sizes, tiles, users, positives, codes, shift,
-    all_tiles, all_users, own_positives, all_shift, sends, recvs, locals_,
+    all_tiles, all_users, own_positives, all_shift, zeroed, sends, recvs, locals_, zbuf, zsem,
 ):
     nx, nz, ny, nc = sizes
     x, z, y, c = (lax.axis_index(a) for a in AXES)
@@ -104,6 +105,14 @@
     ]
     for copy in own:
         copy.start()
+    zbuf[...] = jnp.zeros_like(zbuf)
+    piece = zbuf.shape[0]
+    zeros = [
+        pltpu.make_async_copy(zbuf, zeroed.at[pl.ds(k * piece, piece)], zsem.at[k])
+        for k in range(zeroed.shape[0] // piece)
+    ]
+    for copy in zeros:
+        copy.start()
     late = []
     p2 = {}
     for h in (0, 1):
@@ -192,7 +201,7 @@
     onward(2)
     for arrival in late:
         arrival.wait_recv()
-    for copy in own[2:]:
+    for copy in own[2:] + zeros:
         copy.wait()
     for copy in sent:
         copy.wait_send()
@@ -229,21 +238,12 @@
 
 def stats_kernel(
     half, scale, codes, mine, users, tiles, shift_ref,
-    stats, list_ref, zeroed, ubuf, tbuf, zbuf, usem, tsem, zsem,
+    stats, list_ref, ubuf, tbuf, usem, tsem,
 ):
     nw = users.shape[0]
     ny = tiles.shape[0]
     rows = ubuf.shape[1]
     t = mine[0]
-    zbuf[...] = jnp.zeros_like(zbuf)
-    piece = zbuf.shape[0]
-    zeros = [
-        pltpu.make_async_copy(zbuf, zeroed.at[pl.ds(k * piece, piece)], zsem.at[k])
-        for k in range(zeroed.shape[0] // piece)
-    ]
-    for copy in zeros:
-        copy.start()
-
     def gather(w, n):
         for i in range(2):
             for yp in range(ny):
@@ -256,39 +256,40 @@
     list_ref[0, total] = -1
     list_ref[1, total] = 0
     list_ref[2, 0] = total
-    stats[:, 0:1, :] = jnp.full((stats.shape[0], 1, stats.shape[2]), LOW, jnp.float32)
-    stats[:, 1:2, :] = jnp.zeros((stats.shape[0], 1, stats.shape[2]), jnp.float32)
+    stats[:, :, :, 0] = jnp.full(stats.shape[:3] + stats.shape[4:], LOW, jnp.float32)
+    stats[:, :, :, 1] = jnp.zeros(stats.shape[:3] + stats.shape[4:], jnp.float32)
     get = functools.partial(fetch, users, tiles, list_ref, ubuf, tbuf, usem, tsem, half)
 
-    @pl.when(total > 0)
-    def _():
-        for copy in get(0, 0):
-            copy.start()
+    ahead = ubuf.shape[0] - 1
+    for k in range(ahead):
+        @pl.when(total > k)
+        def _():
+            for copy in get(k, k):
+                copy.start()
 
     def step(e, _):
-        slot = e % 2
-
-        @pl.when(e + 1 < total)
+        slot = e % (ahead + 1)
+
+        @pl.when(e + ahead < total)
         def _():
-            for copy in get(e + 1, 1 - slot):
+            for copy in get(e + ahead, (e + ahead) % (ahead + 1)):
                 copy.start()
 
         for copy in get(e, slot):
             copy.wait()
         b, tile = list_ref[0, e], list_ref[1, e]
         _, _, logits = scores(ubuf, tbuf, shift_ref, slot, tile, scale)
-        before = stats[b, 0:1, 0:rows]
-        held = stats[b, 1:2, 0:rows]
+        at = ((b // 2) % 2, b // 4, b % 2)
+        before = stats[at + (0, slice(None), pl.ds(0, rows))]
+        held = stats[at + (1, slice(None), pl.ds(0, rows))]
         top = jnp.maximum(before, jnp.max(logits, axis=0, keepdims=True))
-        stats[b, 0:1, 0:rows] = top
-        stats[b, 1:2, 0:rows] = held * jnp.exp(before - top) + jnp.sum(
+        stats[at + (0, slice(None), pl.ds(0, rows))] = top
+        stats[at + (1, slice(None), pl.ds(0, rows))] = held * jnp.exp(before - top) + jnp.sum(
             jnp.exp(logits - top), axis=0, keepdims=True
         )
         return 0
 
     lax.fori_loop(0, total, step, 0)
-    for copy in zeros:
-        copy.wait()
 
 
 def as_row(column):
@@ -305,55 +306,66 @@
 
 def total_kernel(
     sizes, scale, stats, user, positive, totals, losses, factor,
-    came, mine, got, lost, s1, r1, s2, r2, s3, r3,
+    across, joined, came, mine, got, beside, lost, s0, r0, s1, r1, s2, r2, s3, r3,
 ):
     nx, nz, ny, nc = sizes
     x, z, y, c = (lax.axis_index(a) for a in AXES)
-    nw = nz * nc
-    me = z * nc + c
     rows = user.shape[0] // 2
     barrier = pltpu.get_barrier_semaphore()
+    sibling = {"c": 1 - c}
 
     def there(d):
-        p = lax.rem(me + d, nw)
-        return p, {"z": p // nc, "c": p % nc}
+        p = lax.rem(z + d, nz)
+        return p, {"z": p}
 
     def hello(d, _):
         pl.semaphore_signal(barrier, inc=1, device_id=there(d)[1], device_id_type=MESH)
         return 0
 
-    lax.fori_loop(1, nw, hello, 0)
+    pl.semaphore_signal(barrier, inc=1, device_id=sibling, device_id_type=MESH)
+    lax.fori_loop(1, nz, hello, 0)
     for d in range(1, nx):
         pl.semaphore_signal(
             barrier, inc=1, device_id={"x": lax.rem(x + d, nx)}, device_id_type=MESH
         )
-    pl.semaphore_wait(barrier, nw - 1 + nx - 1)
-
-    def out(d, _):
-        p, where = there(d)
-        remote(stats.at[p], came.at[me], s1, r1, d, where).start()
-        return 0
-
-    lax.fori_loop(1, nw, out, 0)
+    pl.semaphore_wait(barrier, nz - 1 + nx - 1 + 1)
+
+    over = remote(stats.at[1 - c], across, s0, r0, 0, sibling)
+    over.start()
     dots = []
     for i in range(2):
         u = user[i * rows:(i + 1) * rows].astype(jnp.float32)
         v = positive[i * rows:(i + 1) * rows].astype(jnp.float32)
         dots.append(as_row(jnp.sum(u * v, axis=1, keepdims=True)) * scale)
-
-    def landed(d, _):
-        p, where = there(nw - d)
-        remote(came.at[p], came.at[p], s1, r1, d, where).wait_recv()
+    over.wait_recv()
+    here = stats[pl.ds(c, 1)][0]
+    there_ = across[...]
+    tops = jnp.maximum(here[:, :, 0], there_[:, :, 0])
+    joined[:, :, 0] = tops
+    joined[:, :, 1] = here[:, :, 1] * jnp.exp(here[:, :, 0] - tops) + there_[:, :, 1] * jnp.exp(
+        there_[:, :, 0] - tops
+    )
+
+    def out(d, _):
+        p, where = there(d)
+        remote(joined.at[p], came.at[z], s1, r1, d, where).start()
         return 0
 
-    lax.fori_loop(1, nw, landed, 0)
-    came[pl.ds(me, 1)] = stats[pl.ds(me, 1)]
+    lax.fori_loop(1, nz, out, 0)
     mine[...] = jnp.zeros_like(mine)
     factor[...] = jnp.zeros_like(factor)
     lost[pl.ds(x, 1)] = jnp.zeros((1,) + lost.shape[1:], jnp.float32)
+    came[pl.ds(z, 1)] = joined[pl.ds(z, 1)]
+
+    def landed(d, _):
+        p, where = there(nz - d)
+        remote(came.at[p], came.at[p], s1, r1, d, where).wait_recv()
+        return 0
+
+    lax.fori_loop(1, nz, landed, 0)
     for i in range(2):
-        tops = came[:, i, 0:1, 0:rows]
-        sums = came[:, i, 1:2, 0:rows]
+        tops = came[:, i, 0, :, 0:rows]
+        sums = came[:, i, 1, :, 0:rows]
         ceiling = jnp.maximum(jnp.max(tops, axis=0), dots[i])
         whole = jnp.sum(sums * jnp.exp(tops - ceiling[None]), axis=0) + jnp.exp(dots[i] - ceiling)
         log_total = ceiling + jnp.log(whole)
@@ -363,40 +375,46 @@
 
     def back(d, _):
         _, where = there(d)
-        remote(mine, got.at[me], s2, r2, d, where).start()
+        remote(mine, got.at[z], s2, r2, d, where).start()
         return 0
 
-    lax.fori_loop(1, nw, back, 0)
+    lax.fori_loop(1, nz, back, 0)
     for d in range(1, nx):
         remote(lost.at[x], lost.at[x], s3, r3, d, {"x": lax.rem(x + d, nx)}).start()
-    got[pl.ds(me, 1)] = mine[...][None]
+    got[pl.ds(z, 1)] = mine[...][None]
 
     def done(d, _):
-        p, where = there(nw - d)
+        p, where = there(nz - d)
         remote(got.at[p], got.at[p], s2, r2, d, where).wait_recv()
         return 0
 
-    lax.fori_loop(1, nw, done, 0)
-    totals[...] = got[...]
+    lax.fori_loop(1, nz, done, 0)
+    give = remote(got, beside, s0, r0, 1, sibling)
+    give.start()
+    totals[pl.ds(c, 1)] = got[...][None]
     for d in range(1, nx):
         frm = lax.rem(x - d + nx, nx)
         remote(lost.at[frm], lost.at[frm], s3, r3, d, {"x": frm}).wait_recv()
     losses[...] = lost[...]
+    give.wait_recv()
+    totals[pl.ds(1 - c, 1)] = beside[...][None]
 
     def left(d, _):
         p, where = there(d)
-        remote(stats.at[p], came.at[me], s1, r1, d, where).wait_send()
-        remote(mine, got.at[me], s2, r2, d, where).wait_send()
+        remote(joined.at[p], came.at[z], s1, r1, d, where).wait_send()
+        remote(mine, got.at[z], s2, r2, d, where).wait_send()
         return 0
 
-    lax.fori_loop(1, nw, left, 0)
+    lax.fori_loop(1, nz, left, 0)
     for d in range(1, nx):
         remote(lost.at[x], lost.at[x], s3, r3, d, {"x": lax.rem(x + d, nx)}).wait_send()
+    over.wait_send()
+    give.wait_send()
 
 
 def grads_kernel(
     half, scale, list_ref, users, tiles, shift_ref, totals, _zeroed,
-    grads, cluster, ubuf, tbuf, acc, gout, usem, tsem, gsem,
+    grads, cluster, ubuf, tbuf, usem, tsem, acc, gout, gsem,
 ):
     rows = ubuf.shape[1]
     parts = tbuf.shape[1]
@@ -404,20 +422,22 @@
     cluster[...] = jnp.zeros_like(cluster)
     get = functools.partial(fetch, users, tiles, list_ref, ubuf, tbuf, usem, tsem, half)
 
-    @pl.when(total > 0)
-    def _():
-        for copy in get(0, 0):
-            copy.start()
+    ahead = ubuf.shape[0] - 1
+    for k in range(ahead):
+        @pl.when(total > k)
+        def _():
+            for copy in get(k, k):
+                copy.start()
 
     def put(b, slot):
         return pltpu.make_async_copy(gout.at[slot], grads.at[b], gsem.at[slot])
 
     def step(e, n):
-        slot = e % 2
-
-        @pl.when(e + 1 < total)
+        slot = e % (ahead + 1)
+
+        @pl.when(e + ahead < total)
         def _():
-            for copy in get(e + 1, 1 - slot):
+            for copy in get(e + ahead, (e + ahead) % (ahead + 1)):
                 copy.start()
 
         for copy in get(e, slot):
@@ -426,7 +446,7 @@
         fresh = jnp.logical_or(e == 0, list_ref[0, jnp.maximum(e - 1, 0)] != b)
         last = list_ref[0, e + 1] != b
         user, ads, logits = scores(ubuf, tbuf, shift_ref, slot, tile, scale)
-        probs = jnp.exp(logits - totals[b, :, 0:rows]).astype(jnp.bfloat16)
+        probs = jnp.exp(logits - totals[(b // 2) % 2, b // 4, b % 2, :, 0:rows]).astype(jnp.bfloat16)
         wide = probs.astype(jnp.float32).reshape(parts, probs.shape[0] // parts, rows)
         mass = jnp.sum(wide, axis=1).astype(jnp.bfloat16)
         slots = jnp.dot(mass, user, preferred_element_type=jnp.float32)
@@ -463,8 +483,8 @@
 
 def return_kernel(
     sizes, factor_scale, grads, cluster, factor, positive, user_grad, centroid_grad,
-    own, sib, up_out, up_in, down_out, down_in, final, landed, parts,
-    own_sem, sib_s, sib_r, up_s, up_r, down_s, down_r, fin_s, fin_r, cl_s, cl_r,
+    own, sib, long_out, long_in, short_out, short_in, final, landed, parts,
+    own_sem, sib_s, sib_r, long_s, long_r, short_s, short_r, fin_s, fin_r, cl_s, cl_r,
 ):
     nx, nz, ny, nc = sizes
     x, z, y, c = (lax.axis_index(a) for a in AXES)
@@ -482,8 +502,8 @@
     order = []
     for s in range(steps):
         order.append(steps - s)
-        if s < steps - 1:
-            order.append(s + 1 - steps)
+        if s > 0:
+            order.append(s - steps)
     order.append(0)
     loads, crossing = {}, {}
     for k, d in enumerate(order):
@@ -509,34 +529,41 @@
         loads[d].wait()
         crossing[d].wait_recv()
 
-    ups = lambda s, i: remote(up_out.at[s, i], up_in.at[s, i], up_s, up_r, 2 * s + i, above)
-    downs = lambda s, i: remote(down_out.at[s, i], down_in.at[s, i], down_s, down_r, 2 * s + i, below)
+    away = lambda i: above if i == 0 else below
+    back = lambda i: below if i == 0 else above
+    longs = lambda s, i: remote(
+        long_out.at[s, i], long_in.at[s, i], long_s, long_r, 2 * s + i, away(i)
+    )
+    shorts = lambda s, i: remote(
+        short_out.at[s - 1, i], short_in.at[s - 1, i], short_s, short_r, 2 * s + i, back(i)
+    )
     for s in range(steps):
         ready(steps - s)
-        if s < steps - 1:
-            ready(s + 1 - steps)
+        if s > 0:
+            ready(s - steps)
         for i in range(2):
-            value = both(steps - s, i)
+            sign = 1 if i == 0 else -1
+            value = both(sign * (steps - s) if s > 0 else steps, i)
             if s > 0:
-                ups(s - 1, i).wait_recv()
-                value = value + up_in[s - 1, i].astype(jnp.float32)
-            up_out[s, i] = value.astype(jnp.bfloat16)
-            ups(s, i).start()
-            if s < steps - 1:
-                value = both(s + 1 - steps, i)
-                if s > 0:
-                    downs(s - 1, i).wait_recv()
-                    value = value + down_in[s - 1, i].astype(jnp.float32)
-                down_out[s, i] = value.astype(jnp.bfloat16)
-                downs(s, i).start()
+                longs(s - 1, i).wait_recv()
+                value = value + long_in[s - 1, i].astype(jnp.float32)
+            long_out[s, i] = value.astype(jnp.bfloat16)
+            longs(s, i).start()
+            if s > 0:
+                value = both(sign * (s - steps), i)
+                if s > 1:
+                    shorts(s - 1, i).wait_recv()
+                    value = value + short_in[s - 2, i].astype(jnp.float32)
+                short_out[s - 1, i] = value.astype(jnp.bfloat16)
+                shorts(s, i).start()
     ready(0)
     for i in range(2):
-        downs(steps - 2, i).wait_recv()
-        ups(steps - 1, i).wait_recv()
+        shorts(steps - 1, i).wait_recv()
+        longs(steps - 1, i).wait_recv()
         value = (
             both(0, i)
-            + up_in[steps - 1, i].astype(jnp.float32)
-            + down_in[steps - 2, i].astype(jnp.float32)
+            + long_in[steps - 1, i].astype(jnp.float32)
+            + short_in[steps - 2, i].astype(jnp.float32)
         )
         wide = positive[i * rows:(i + 1) * rows].astype(jnp.float32)
         value = (value + as_column(factor[i, :, 0:rows]) * wide) * factor_scale
@@ -562,9 +589,9 @@
         copy.wait_send()
     for i in range(2):
         for s in range(steps):
-            ups(s, i).wait_send()
-        for s in range(steps - 1):
-            downs(s, i).wait_send()
+            longs(s, i).wait_send()
+        for s in range(1, steps):
+            shorts(s, i).wait_send()
 
 
 def params(identity=None, megabytes=48):
@@ -572,6 +599,89 @@
         collective_id=identity,
         has_side_effects=identity is not None,
         vmem_limit_bytes=megabytes * 1024 * 1024,
+    )
+
+
+def lanes_of(rows):
+    return -(-rows // 128) * 128
+
+
+def buffers_of(rows, width, nx, quarter):
+    return [
+        pltpu.VMEM((SLOTS, rows, width), jnp.bfloat16),
+        pltpu.VMEM((SLOTS, nx, quarter, width), jnp.bfloat16),
+        pltpu.SemaphoreType.DMA((SLOTS,)),
+        pltpu.SemaphoreType.DMA((SLOTS,)),
+    ]
+
+
+def stats_call(nw, ny, half, scale, rows, width, nx, quarter):
+    sds = jax.ShapeDtypeStruct
+    return pl.pallas_call(
+        functools.partial(stats_kernel, half, scale),
+        out_shape=(
+            sds((2, nw // 2, 2, 2, 1, lanes_of(rows)), jnp.float32),
+            sds((3, nw * ny + 8), jnp.int32),
+        ),
+        in_specs=[SMEM, SMEM, HBM, HBM, VMEM],
+        out_specs=[VMEM, SMEM],
+        scratch_shapes=buffers_of(rows, width, nx, quarter),
+        compiler_params=params(None, 58),
+        name="stats",
+    )
+
+
+def grads_call(nw, ny, half, scale, rows, width, nx, quarter):
+    sds = jax.ShapeDtypeStruct
+    return pl.pallas_call(
+        functools.partial(grads_kernel, half, scale),
+        out_shape=(
+            sds((2 * nw, rows, width), jnp.bfloat16),
+            sds((2 * ny * half, 1, width), jnp.float32),
+        ),
+        in_specs=[SMEM, HBM, HBM, VMEM, VMEM, HBM],
+        out_specs=[HBM, VMEM],
+        input_output_aliases={5: 0},
+        scratch_shapes=buffers_of(rows, width, nx, quarter)
+        + [
+            pltpu.VMEM((rows, width), jnp.float32),
+            pltpu.VMEM((2, rows, width), jnp.bfloat16),
+            pltpu.SemaphoreType.DMA((2,)),
+        ],
+        compiler_params=params(None, 58),
+        name="grads",
+    )
+
+
+def totals_call(sizes, scale, rows):
+    nx, nz, ny, nc = sizes
+    lanes = lanes_of(rows)
+    sds = lambda *shape: jax.ShapeDtypeStruct(shape, jnp.float32)
+    buffer = lambda *shape: pltpu.VMEM(shape, jnp.float32)
+    dma = pltpu.SemaphoreType.DMA
+    return pl.pallas_call(
+        functools.partial(total_kernel, sizes, scale),
+        out_shape=(
+            sds(nc, nz, 2, 1, lanes),
+            sds(nx, 2, 1, lanes),
+            sds(2, 1, lanes),
+        ),
+        in_specs=[VMEM] * 3,
+        out_specs=[VMEM] * 3,
+        scratch_shapes=[
+            buffer(nz, 2, 2, 1, lanes),
+            buffer(nz, 2, 2, 1, lanes),
+            buffer(nz, 2, 2, 1, lanes),
+            buffer(2, 1, lanes),
+            buffer(nz, 2, 1, lanes),
+            buffer(nz, 2, 1, lanes),
+            buffer(nx, 2, 1, lanes),
+        ]
+        + [dma((2,))] * 2
+        + [dma((nz,))] * 4
+        + [dma((nx,))] * 2,
+        compiler_params=params(1, 24),
+        name="totals",
     )
 
 
@@ -611,18 +721,22 @@
     steps = nz // 2
     copies = 2 * (nx - 1) + (ny - 1) + 8 + 4 + 12 + 16 + (nz - 1) + nz
     mine = 2 * rows
-    all_tiles, all_users, positives, all_shift = pl.pallas_call(
+    all_tiles, all_users, positives, all_shift, zeroed = pl.pallas_call(
         functools.partial(gather_kernel, sizes),
         out_shape=(
             sds((ny, nx, 2, half, quarter, width), bf16),
             sds((nz, nc, mine + CODE_ROWS, width), bf16),
             sds((mine, width), bf16),
             sds((ny, per, tile), bf16),
+            sds((2 * nw, rows, width), bf16),
         ),
         in_specs=[HBM] * 5,
-        out_specs=[HBM] * 4,
-        scratch_shapes=[dma((copies,)), dma((copies,)), dma((5,))],
-        compiler_params=params(0, 4),
+        out_specs=[HBM] * 5,
+        scratch_shapes=[
+            dma((copies,)), dma((copies,)), dma((5,)),
+            pltpu.VMEM((4, rows, width), bf16), dma((nw // 2,)),
+        ],
+        compiler_params=params(0, 58),
         name="gather",
     )(ad_rows.reshape(2, half, quarter, width), user_rows, positive_rows, codes, shift)
 
@@ -632,59 +746,16 @@
     places = jnp.swapaxes(picked, 0, 1).reshape(2, nw * ny).astype(jnp.int32)
     flat_users = all_users.reshape(nw, mine + CODE_ROWS, width)
     flat_shift = all_shift.reshape(ny * per, tile)
-    lanes = -(-rows // 128) * 128
-    buffers = [pltpu.VMEM((2, rows, width), bf16), pltpu.VMEM((2, nx, quarter, width), bf16)]
-    stats, entries, zeroed = pl.pallas_call(
-        functools.partial(stats_kernel, half, scale),
-        out_shape=(
-            sds((2 * nw, 2, lanes), f32),
-            sds((3, nw * ny + 8), jnp.int32),
-            sds((2 * nw, rows, width), bf16),
-        ),
-        in_specs=[SMEM, SMEM, HBM, HBM, VMEM],
-        out_specs=[VMEM, SMEM, HBM],
-        scratch_shapes=buffers
-        + [pltpu.VMEM((4, rows, width), bf16), dma((2,)), dma((2,)), dma((nw // 2,))],
-        compiler_params=params(),
-        name="stats",
-    )(places, x.astype(jnp.int32).reshape(1), flat_users, all_tiles, flat_shift)
+    stats, entries = stats_call(nw, ny, half, scale, rows, width, nx, quarter)(
+        places, x.astype(jnp.int32).reshape(1), flat_users, all_tiles, flat_shift
+    )
 
     own_users = lax.dynamic_index_in_dim(flat_users, z * nc + c, 0, keepdims=False)[:mine]
-    totals, losses, factor = pl.pallas_call(
-        functools.partial(total_kernel, sizes, scale),
-        out_shape=(
-            sds((nw, 2, 1, lanes), f32),
-            sds((nx, 2, 1, lanes), f32),
-            sds((2, 1, lanes), f32),
-        ),
-        in_specs=[VMEM] * 3,
-        out_specs=[VMEM] * 3,
-        scratch_shapes=[
-            pltpu.VMEM((nw, 2, 2, lanes), f32),
-            pltpu.VMEM((2, 1, lanes), f32),
-            pltpu.VMEM((nw, 2, 1, lanes), f32),
-            pltpu.VMEM((nx, 2, 1, lanes), f32),
-        ]
-        + [dma((nw,))] * 4
-        + [dma((nx,))] * 2,
-        compiler_params=params(1, 24),
-        name="totals",
-    )(stats.reshape(nw, 2, 2, lanes), own_users, positives)
-
-    grads, cluster = pl.pallas_call(
-        functools.partial(grads_kernel, half, scale),
-        out_shape=(sds((2 * nw, rows, width), bf16), sds((ny * per, 1, width), f32)),
-        in_specs=[SMEM, HBM, HBM, VMEM, VMEM, HBM],
-        out_specs=[HBM, VMEM],
-        input_output_aliases={5: 0},
-        scratch_shapes=buffers
-        + [
-            pltpu.VMEM((rows, width), f32), pltpu.VMEM((2, rows, width), bf16),
-            dma((2,)), dma((2,)), dma((2,)),
-        ],
-        compiler_params=params(),
-        name="grads",
-    )(entries, flat_users, all_tiles, flat_shift, totals.reshape(2 * nw, 1, lanes), zeroed)
+    totals, losses, factor = totals_call(sizes, scale, rows)(stats, own_users, positives)
+
+    grads, cluster = grads_call(nw, ny, half, scale, rows, width, nx, quarter)(
+        entries, flat_users, all_tiles, flat_shift, totals, zeroed
+    )
 
     depth = width // nx
     cluster = jnp.swapaxes(cluster.reshape(ny, per, nx, depth), 1, 2)

time: 382 us -> 357 us (0.935)
  Pallas kernels: 352 us -> 335 us
  local copies, waits for them, and re-layouts: 21.4 us -> 11.1 us
    pallas_call x3, Pallas kernels: 71.4 us -> 55.8 us  [the longest x1 29.2 us: local(): totals_call(sizes, scale, rows)(stats, own_users, positives)]
    unnamed x11 -> x9, local copies, waits for them, and re-layouts: 17.3 us -> 3.12 us
where the time goes in v2:
time: 357 us; the launch traced here: 354 us
  Pallas kernels  335 us (94%)
  local copies, waits for them, and re-layouts  11.1 us (3%)
  other arithmetic  7.48 us (2%)
    pallas_call x1, Pallas kernels, local(): pl.pallas_call(functools.partial(gather_kernel, sizes), out_shape=(sds((n...  192 us
    pallas_call x1, Pallas kernels, local(): pl.pallas_call(functools.partial(return_kernel, sizes, LOSS_SCALE * scale...  86.8 us
    pallas_call x1, Pallas kernels, local(): totals_call(sizes, scale, rows)(stats, own_users, positives)  29.2 us
    pallas_call x1, Pallas kernels, local(): grads_call(nw, ny, half, scale, rows, width, nx, quarter)  15.2 us
    pallas_call x1, Pallas kernels, local(): stats_call(nw, ny, half, scale, rows, width, nx, quarter)  11.3 us

profile of v2, /device:TPU:1, one launch (start us, length us, event | category | flops | bytes accessed | tf_op | source)
XLA Modules:
  0.0 354.4 jit_solution(12810386066881693300)
XLA Ops:
  0.6 0.8 broadcast_in_dim_reshape.4
  1.4 0.7 convert_element_type.36
  2.1 0.9 convert_reduce_fusion
  3.0 0.7 fusion
  3.7 0.1 select_n.57
  3.8 0.1 select_reduce_fusion.1
  3.9 1.5 log_convert_fusion.shift
  5.4 0.6 pad.4.codes
  6.0 3.5 add_convert_fusion
  9.5 192.4 %gather.1 = (bf16[4,4,2,16,64,512]{5,4,3,2,1,0:T(8,128)(2,1)}, bf16[16,2,400,512]{3,2,1,0:T(8,128)(2,1)}, bf16[384,512]{1,0:T(8,128)(2,1)}, bf16[4,32,256]{2,1,0:T(8,128)(2,1)}, bf16[64,192,512]{2,1,0:T(8,128)(2,1)}) custom-call(bf16[2,16,64,512]{3,2,1,0:T(8,128)(2,1)} %bitcast.24, bf16[1536,128]{1,0:T(8,128)(2,1)} %users.1, bf16[1536,128]{1,0:T(8,128)(2,1)} %positives.1, ...), custom_call_target="tpu_custom_call" | custom-call | tf_op jit(solution)/shard_map/gather/pallas_call | solution.py:724
  201.9 0.9 slice.12
  202.8 1.0 dynamic-slice_bitcast_fusion.user
  203.8 2.2 reshape.170
  206.1 0.1 dynamic-slice_convert_fusion
  206.2 0.1 copy.21
  206.3 0.1 copy.17
  206.4 0.7 reshape.168.codes
  207.1 0.0 copy-start
  207.1 11.3 %stats.1 = (f32[2,16,2,2,1,256]{5,4,3,2,1,0:T(1,128)}, s32[3,136]{1,0:T(4,128)}) custom-call(s32[2,128]{1,0:T(2,128)} %reshape.168.codes, s32[1]{0:T(128)} %bitcast.5.mine, bf16[32,400,512]{2,1,0:T(8,128)(2,1)} %bitcast.21, bf16[4,4,2,16,64,512]{5,4,3,2,1,0:T(8,128)(2,1)} %get-tuple-element.18.tiles, bf16[128,256]{1,0:T(8,128)(2,1)} %bitcast.26), custom_call_target="tpu_custom_call" | custom-call | tf_op jit(solution)/shard_map/stats/pallas_call | solution.py:749
  218.4 0.0 copy-done
  218.4 0.0 copy-start.1
  218.4 0.9 copy-done.1
  219.3 29.2 %totals.1 = (f32[2,16,2,1,256]{4,3,2,1,0:T(1,128)S(1)}, f32[4,2,1,256]{3,2,1,0:T(1,128)S(1)}, f32[2,1,256]{2,1,0:T(1,128)S(1)}) custom-call(f32[2,16,2,2,1,256]{5,4,3,2,1,0:T(1,128)S(1)} %copy-done.1, bf16[384,512]{1,0:T(8,128)(2,1)S(1)} %dynamic-slice_bitcast_fusion.user, bf16[384,512]{1,0:T(8,128)(2,1)S(1)} %copy-done), custom_call_target="tpu_custom_call" | custom-call | tf_op jit(solution)/shard_map/totals/pallas_call | solution.py:754
  248.5 0.0 copy-start.2
  248.6 0.6 copy-done.2
  249.2 15.2 %grads.1 = (bf16[64,192,512]{2,1,0:T(8,128)(2,1)}, f32[128,1,512]{2,1,0:T(1,128)}) custom-call(s32[3,136]{1,0:T(4,128)} %get-tuple-element.23.list_ref, bf16[32,400,512]{2,1,0:T(8,128)(2,1)} %bitcast.22, bf16[4,4,2,16,64,512]{5,4,3,2,1,0:T(8,128)(2,1)} %get-tuple-element.18.tiles, bf16[128,256]{1,0:T(8,128)(2,1)} %bitcast.27, ...), custom_call_target="tpu_custom_call", output_to_operand_aliasing={{0}: (5, {})} | custom-call | tf_op jit(solution)/shard_map/grads/pallas_call | solution.py:756
  264.4 0.7 reshape_squeeze.3
  265.1 1.0 copy.23
  266.1 86.8 %return.1 = (f32[4,384,128]{2,1,0:T(8,128)S(1)}, f32[32,128]{1,0:T(8,128)S(1)}) custom-call(bf16[16,2,2,192,512]{4,3,2,1,0:T(8,128)(2,1)} %bitcast.23, f32[4,4,32,128]{3,2,1,0:T(8,128)S(1)} %bitcast.18, f32[2,1,256]{2,1,0:T(1,128)S(1)} %get-tuple-element.28.factor, bf16[384,512]{1,0:T(8,128)(2,1)S(1)} %copy-done), custom_call_target="tpu_custom_call" | custom-call | tf_op jit(solution)/shard_map/return/pallas_call | solution.py:763
  352.9 0.9 copy.27
  353.8 0.6 copy.28
  (5 shorter events, 0.1 us)
Async XLA Ops:
  207.1 11.3 %copy-start = (bf16[384,512]{1,0:T(8,128)(2,1)S(1)}, bf16[384,512]{1,0:T(8,128)(2,1)}, u32[]{:S(2)}) copy-start(bf16[384,512]{1,0:T(8,128)(2,1)} %get-tuple-element.21.positive) | copy-start | bytes 1179652
  218.4 0.9 copy-start.1
  248.5 0.6 copy-start.2

commit v3 on v2

v3 whole, which is shorter than its diff:
```python
import functools
import math

import jax
import jax.numpy as jnp
from jax import lax
from jax.experimental import pallas as pl
from jax.experimental.pallas import tpu as pltpu
from jax.sharding import Mesh, PartitionSpec as P

LOSS_SCALE = 16
AXES = ("x", "z", "y", "c")
SPLIT = (16, 4, 2)
LOW = -1e30
LOG2E = math.log2(math.e)
LN2 = math.log(2.0)
MESH = pl.DeviceIdType.MESH
HBM = pl.BlockSpec(memory_space=pl.ANY)
VMEM = pl.BlockSpec(memory_space=pltpu.VMEM)
SMEM = pl.BlockSpec(memory_space=pltpu.SMEM)
CODE_ROWS = 16
SLOTS = 8
MASS_ROWS = 8


def remote(src, dst, sends, recvs, k, where):
    return pltpu.make_async_remote_copy(
        src_ref=src,
        dst_ref=dst,
        send_sem=sends.at[k],
        recv_sem=recvs.at[k],
        device_id=where,
        device_id_type=MESH,
    )


def greet(peers):
    barrier = pltpu.get_barrier_semaphore()
    for where in peers:
        pl.semaphore_signal(barrier, inc=1, device_id=where, device_id_type=MESH)
    pl.semaphore_wait(barrier, len(peers))


def gather_kernel(
    sizes, tiles, users, positives, codes, shift,
    all_tiles, all_users, own_positives, all_shift, zeroed, sends, recvs, locals_, zbuf, zsem,
):
    nx, nz, ny, nc = sizes
    x, z, y, c = (lax.axis_index(a) for a in AXES)
    rows = users.shape[0] // nx
    depth = users.shape[1]
    half = tiles.shape[1]
    quarter = half // 2
    at_x = lambda d: lax.rem(x + d + nx, nx)
    at_y = lambda d: lax.rem(y + d + ny, ny)
    at_z = lambda d: lax.rem(z + d + nz, nz)
    to_x = lambda d: {"x": at_x(d)}
    to_y = lambda d: {"y": at_y(d)}
    to_z = lambda d: {"z": at_z(d)}
    sibling = {"c": 1 - c}

    greet(
        [to_x(d) for d in range(1, nx)]
        + [to_y(d) for d in range(1, ny)]
        + [to_z(1), to_z(-1), sibling]
    )

    count = [0]
    sent = []

    def push(src, dst, where, landing):
        k = count[0]
        count[0] += 1
        copy = remote(src, dst, sends, recvs, k, where)
        copy.start()
        sent.append(copy)
        return remote(landing, landing, sends, recvs, k, where)

    columns = lambda i: pl.ds(pl.multiple_of(i * depth, depth), depth)
    part = lambda i: pl.ds(pl.multiple_of(i * rows, rows), rows)
    home = all_users.at[z, c]

    def block(h, a, b):
        return all_tiles.at[at_y(b), at_x(a), h] if h == 0 else all_tiles.at[at_y(a), at_x(b), h]

    first = (to_x, to_y)
    second = (to_y, to_x)
    lower, upper = pl.ds(0, quarter), pl.ds(quarter, quarter)

    arrivals = []
    for d in range(1, nx):
        arrivals.append(
            push(
                users.at[part(at_x(d))], home.at[pl.ds(0, rows), columns(x)], to_x(d),
                home.at[pl.ds(0, rows), columns(at_x(-d))],
            )
        )
    p1 = {}
    for h in (0, 1):
        for d in (1, -1):
            p1[h, d] = push(tiles.at[h], block(h, 0, 0), first[h](d), block(h, -d, 0))
    own = [
        pltpu.make_async_copy(users.at[part(x)], home.at[pl.ds(0, rows), columns(x)], locals_.at[0]),
        pltpu.make_async_copy(codes, home.at[pl.ds(rows, CODE_ROWS)], locals_.at[1]),
        pltpu.make_async_copy(tiles, all_tiles.at[y, x], locals_.at[2]),
        pltpu.make_async_copy(shift, all_shift.at[y], locals_.at[3]),
        pltpu.make_async_copy(positives.at[part(x)], own_positives.at[:, columns(x)], locals_.at[4]),
    ]
    for copy in own:
        copy.start()
    zbuf[...] = jnp.zeros_like(zbuf)
    piece = zbuf.shape[0]
    zeros = [
        pltpu.make_async_copy(zbuf, zeroed.at[pl.ds(k * piece, piece)], zsem.at[k])
        for k in range(zeroed.shape[0] // piece)
    ]
    for copy in zeros:
        copy.start()
    late = []
    p2 = {}
    for h in (0, 1):
        for d in (1, -1):
            p2[h, 0, d] = push(tiles.at[h], block(h, 0, 0), second[h](d), block(h, 0, -d))
    for d in range(1, nx):
        late.append(
            push(
                positives.at[part(at_x(d))], own_positives.at[:, columns(x)], to_x(d),
                own_positives.at[:, columns(at_x(-d))],
            )
        )
    for d in range(1, ny):
        late.append(push(shift, all_shift.at[y], to_y(d), all_shift.at[at_y(-d)]))

    for arrival in arrivals:
        arrival.wait_recv()
    own[0].wait()
    own[1].wait()

    chunk = lambda d: all_users.at[at_z(d), c]
    other = lambda d: all_users.at[at_z(d), 1 - c]
    steps = nz // 2
    up, down = {}, {}

    def ring(s):
        if s > 0:
            up[s - 1].wait_recv()
            if s - 1 in down:
                down[s - 1].wait_recv()
        if s < steps:
            up[s] = push(chunk(-s), chunk(-s), to_z(1), chunk(-s - 1))
        if s < steps - 1:
            down[s] = push(chunk(s), chunk(s), to_z(-1), chunk(s + 1))
        late.append(push(chunk(-s), chunk(-s), sibling, other(-s)))
        if 0 < s < steps:
            late.append(push(chunk(s), chunk(s), sibling, other(s)))

    turns = list(range(steps + 1))
    ring(turns.pop(0))
    while len(turns) > steps - 3 and turns:
        ring(turns.pop(0))

    for h in (0, 1):
        for d in (1, -1):
            p1[h, d].wait_recv()
    q = {}
    for h in (0, 1):
        for d in (1, -1):
            cut = lower if d == 1 else upper
            q[h, d] = push(
                block(h, -d, 0).at[cut], block(h, -d, 0).at[cut], first[h](d), block(h, -2 * d, 0).at[cut]
            )
    for j in (1, -1):
        for h in (0, 1):
            for d in (1, -1):
                p2[h, j, d] = push(block(h, j, 0), block(h, j, 0), second[h](d), block(h, j, -d))
    if turns:
        ring(turns.pop(0))

    def onward(j):
        for h in (0, 1):
            for d in (1, -1):
                p2[h, j, d].wait_recv()
                cut = lower if d == 1 else upper
                late.append(
                    push(
                        block(h, j, -d).at[cut], block(h, j, -d).at[cut], second[h](d),
                        block(h, j, -2 * d).at[cut],
                    )
                )

    onward(0)
    for h in (0, 1):
        for d in (1, -1):
            q[h, d].wait_recv()
    for h in (0, 1):
        for d in (1, -1):
            p2[h, 2, d] = push(block(h, 2, 0), block(h, 2, 0), second[h](d), block(h, 2, -d))
    if turns:
        ring(turns.pop(0))
    onward(1)
    while turns:
        ring(turns.pop(0))
    onward(-1)
    onward(2)
    for arrival in late:
        arrival.wait_recv()
    for copy in own[2:] + zeros:
        copy.wait()
    for copy in sent:
        copy.wait_send()
    assert count[0] == sends.shape[0], count[0]


def fetch(users, tiles, list_ref, ubuf, tbuf, usem, tsem, half, e, slot):
    b, tile = list_ref[0, e], list_ref[1, e]
    per = 2 * half
    yp, cl = tile // per, tile % per
    w, i = b // 2, b % 2
    rows = ubuf.shape[1]
    return (
        pltpu.make_async_copy(
            users.at[w, pl.ds(pl.multiple_of(i * rows, rows), rows)], ubuf.at[slot], usem.at[slot]
        ),
        pltpu.make_async_copy(
            tiles.at[yp, :, cl // half, cl % half], tbuf.at[slot], tsem.at[slot]
        ),
    )


def scores(ubuf, tbuf, shift_ref, slot, tile, scale):
    user = ubuf[slot]
    ads = tbuf[slot].reshape(tbuf.shape[1] * tbuf.shape[2], tbuf.shape[3])
    pick = lax.broadcasted_iota(jnp.int32, (shift_ref.shape[0], user.shape[0]), 0) == tile
    shift = lax.dot_general(
        shift_ref[...], pick.astype(jnp.float32).astype(jnp.bfloat16), (((0,), (0,)), ((), ())),
        preferred_element_type=jnp.float32,
    )
    raw = lax.dot_general(ads, user, (((1,), (1,)), ((), ())), preferred_element_type=jnp.float32)
    return user, ads, raw * scale - shift


def flash_kernel(
    half, scale, codes, mine, users, tiles, shift_ref, _zeroed,
    stats, masses, grads, list_ref, ubuf, tbuf, usem, tsem, acc, gout, gsem,
):
    nw = users.shape[0]
    ny = tiles.shape[0]
    rows = ubuf.shape[1]
    parts = tbuf.shape[1]
    t = mine[0]

    def gather(w, n):
        for i in range(2):
            for yp in range(ny):
                list_ref[0, n] = w * 2 + i
                list_ref[1, n] = yp * (2 * half) + codes[1, w * ny + yp]
                n = n + (codes[0, w * ny + yp] == 2 * t + i).astype(jnp.int32)
        return n

    total = lax.fori_loop(0, nw, gather, jnp.int32(0))
    list_ref[0, total] = -1
    list_ref[1, total] = 0
    get = functools.partial(fetch, users, tiles, list_ref, ubuf, tbuf, usem, tsem, half)
    ahead = ubuf.shape[0] - 1
    for k in range(ahead):
        @pl.when(total > k)
        def _():
            for copy in get(k, k):
                copy.start()

    stats[:, :, :, 0] = jnp.full(stats.shape[:3] + stats.shape[4:], LOW, jnp.float32)
    stats[:, :, :, 1] = jnp.zeros(stats.shape[:3] + stats.shape[4:], jnp.float32)
    masses[...] = jnp.zeros_like(masses)

    def put(b, slot):
        return pltpu.make_async_copy(gout.at[slot], grads.at[b], gsem.at[slot])

    def step(e, n):
        slot = e % (ahead + 1)

        @pl.when(e + ahead < total)
        def _():
            for copy in get(e + ahead, (e + ahead) % (ahead + 1)):
                copy.start()

        for copy in get(e, slot):
            copy.wait()
        b, tile = list_ref[0, e], list_ref[1, e]
        fresh = jnp.logical_or(e == 0, list_ref[0, jnp.maximum(e - 1, 0)] != b)
        last = list_ref[0, e + 1] != b
        at = ((b // 2) % 2, b // 4, b % 2)
        user, ads, logits = scores(ubuf, tbuf, shift_ref, slot, tile, scale)
        logits = logits * LOG2E
        before = stats[at + (0, slice(None), pl.ds(0, rows))]
        held = stats[at + (1, slice(None), pl.ds(0, rows))]
        top = jnp.maximum(before, jnp.ceil(jnp.max(logits, axis=0, keepdims=True)))
        carry = jnp.exp2(before - top)
        terms = jnp.exp2(logits - top)
        stats[at + (0, slice(None), pl.ds(0, rows))] = top
        stats[at + (1, slice(None), pl.ds(0, rows))] = held * carry + jnp.sum(
            terms, axis=0, keepdims=True
        )
        probs = terms.astype(jnp.bfloat16)
        wide = probs.astype(jnp.float32).reshape(parts, probs.shape[0] // parts, rows)
        mass = jnp.sum(wide, axis=1)
        term = lax.dot_general(probs, ads, (((0,), (0,)), ((), ())), preferred_element_type=jnp.float32)

        @pl.when(fresh)
        def _():
            acc[...] = term

        @pl.when(jnp.logical_not(fresh))
        def _():
            acc[...] = acc[...] * as_column(carry) + term
            masses[b, :, :, 0:rows] = masses[b, :, :, 0:rows] * carry[None]

        masses[b, tile // (2 * half), 0:parts, 0:rows] = mass

        @pl.when(last)
        def _():
            to = n % 2

            @pl.when(n >= 2)
            def _():
                put(0, to).wait()

            gout[to] = acc[...].astype(jnp.bfloat16)
            put(b, to).start()

        return n + last.astype(jnp.int32)

    n = lax.fori_loop(0, total, step, jnp.int32(0))
    for k in range(2):
        @pl.when(n > k)
        def _():
            put(0, k).wait()


def as_row(column):
    n = column.shape[0]
    eye = lax.broadcasted_iota(jnp.int32, (n, n), 0) == lax.broadcasted_iota(jnp.int32, (n, n), 1)
    return jnp.sum(jnp.where(eye, column, 0.0), axis=0, keepdims=True)


def as_column(row):
    n = row.shape[1]
    eye = lax.broadcasted_iota(jnp.int32, (n, n), 0) == lax.broadcasted_iota(jnp.int32, (n, n), 1)
    return jnp.sum(jnp.where(eye, row, 0.0), axis=1, keepdims=True)


def diagonal(row):
    n = row.shape[1]
    eye = lax.broadcasted_iota(jnp.int32, (n, n), 0) == lax.broadcasted_iota(jnp.int32, (n, n), 1)
    return jnp.where(eye, row, 0.0).astype(jnp.bfloat16)


def return_kernel(
    sizes, scale, factor_scale, grads, stats, masses, names, users, positive,
    user_grad, centroid_grad, losses,
    own, sib, long_out, long_in, short_out, short_in,
    klong_out, klong_in, kshort_out, kshort_in,
    final, landed, parts, cluster, everyone, terms,
    across, joined, came, mine, got, beside, lost, factor,
    own_sem, sib_s, sib_r, long_s, long_r, short_s, short_r,
    kl_s, kl_r, ks_s, ks_r, fin_s, fin_r, cl_s, cl_r,
    s0, r0, s1, r1, s2, r2, s3, r3, usem,
):
    nx, nz, ny, nc = sizes
    x, z, y, c = (lax.axis_index(a) for a in AXES)
    at_z = lambda d: lax.rem(z + d + nz, nz)
    above, below = {"z": at_z(1)}, {"z": at_z(-1)}
    sibling = {"c": 1 - c}
    rows, width = own.shape[2], own.shape[3]
    per, depth = cluster.shape[2], cluster.shape[3]
    steps = nz // 2
    pairs = [(dx, dy) for dx in range(nx) for dy in range(ny) if dx or dy]
    place = lambda dx, dy: (lax.rem(x + dx + nx, nx), lax.rem(y + dy + ny, ny))
    greet(
        [{"z": at_z(d)} for d in range(1, nz)]
        + [dict(zip(("x", "y"), place(dx, dy))) for dx, dy in pairs]
        + [sibling]
    )
    over = remote(stats.at[1 - c], across, s0, r0, 0, sibling)
    over.start()
    order = []
    for s in range(steps):
        order.append(steps - s)
        if s > 0:
            order.append(s - steps)
    order.append(0)
    index = {d: k for k, d in enumerate(order)}
    loads = [
        pltpu.make_async_copy(grads.at[at_z(d), c], own.at[k], own_sem.at[k])
        for k, d in enumerate(order)
    ]
    crossing = [
        remote(grads.at[at_z(d), 1 - c], sib.at[k], sib_s, sib_r, k, sibling)
        for k, d in enumerate(order)
    ]

    def begin(ks):
        for k in ks:
            loads[k].start()
            crossing[k].start()

    def ready(d):
        loads[index[d]].wait()
        crossing[index[d]].wait_recv()

    def merged(d, i, extra):
        k = index[d]
        items = [
            (stats[c, at_z(d), i, 0, :, pl.ds(0, rows)], own[k, i]),
            (across[at_z(d), i, 0, :, pl.ds(0, rows)], sib[k, i]),
        ] + extra
        top = items[0][0]
        for level, _ in items[1:]:
            top = jnp.maximum(top, level)
        whole = 0.0
        for level, value in items:
            whole = whole + jnp.dot(
                diagonal(jnp.exp2(level - top)), value, preferred_element_type=jnp.float32
            )
        return whole, top

    away = lambda i: above if i == 0 else below
    back = lambda i: below if i == 0 else above
    longs = lambda s, i: (
        remote(long_out.at[s, i], long_in.at[s, i], long_s, long_r, 2 * s + i, away(i)),
        remote(klong_out.at[s, i], klong_in.at[s, i], kl_s, kl_r, 2 * s + i, away(i)),
    )
    shorts = lambda s, i: (
        remote(short_out.at[s - 1, i], short_in.at[s - 1, i], short_s, short_r, 2 * s + i, back(i)),
        remote(kshort_out.at[s - 1, i], kshort_in.at[s - 1, i], ks_s, ks_r, 2 * s + i, back(i)),
    )

    def arrive(copies):
        for copy in copies:
            copy.wait_recv()

    def send_stats():
        begin(range(min(3, nz), nz))
        pltpu.make_async_copy(users.at[:, pl.ds(0, 2 * rows)], everyone, usem.at[0]).start()
        here = stats[pl.ds(c, 1)][0]
        there = across[...]
        tops = jnp.maximum(here[:, :, 0], there[:, :, 0])
        joined[:, :, 0] = tops
        joined[:, :, 1] = here[:, :, 1] * jnp.exp2(here[:, :, 0] - tops) + there[
            :, :, 1
        ] * jnp.exp2(there[:, :, 0] - tops)

        def out(d, _):
            p = lax.rem(z + d, nz)
            remote(joined.at[p], came.at[z], s1, r1, d, {"z": p}).start()
            return 0

        lax.fori_loop(1, nz, out, 0)
        came[pl.ds(z, 1)] = joined[pl.ds(z, 1)]
        mine[...] = jnp.zeros_like(mine)
        factor[...] = jnp.zeros_like(factor)
        lost[pl.ds(x, 1)] = jnp.zeros((1,) + lost.shape[1:], jnp.float32)

    def total():
        pltpu.make_async_copy(users.at[:, pl.ds(0, 2 * rows)], everyone, usem.at[0]).wait()

        def come(d, _):
            p = lax.rem(z + nz - d, nz)
            remote(came.at[p], came.at[p], s1, r1, d, {"z": p}).wait_recv()
            return 0

        lax.fori_loop(1, nz, come, 0)
        for i in range(2):
            u = everyone[z * nc + c, i * rows:(i + 1) * rows].astype(jnp.float32)
            v = positive[i * rows:(i + 1) * rows].astype(jnp.float32)
            dot = as_row(jnp.sum(u * v, axis=1, keepdims=True)) * (scale * LOG2E)
            tops = came[:, i, 0, :, 0:rows]
            sums = came[:, i, 1, :, 0:rows]
            ceiling = jnp.maximum(jnp.max(tops, axis=0), dot)
            whole = jnp.log(
                jnp.sum(sums * jnp.exp2(tops - ceiling[None]), axis=0) + jnp.exp2(dot - ceiling)
            )
            log_total = ceiling + whole * LOG2E
            mine[i, :, 0:rows] = log_total
            lost[pl.ds(x, 1), i, :, 0:rows] = (whole + (ceiling - dot) * LN2)[None]
            factor[i, :, 0:rows] = jnp.exp2(dot - log_total) - 1.0

        def give(d, _):
            p = lax.rem(z + d, nz)
            remote(mine, got.at[z], s2, r2, d, {"z": p}).start()
            return 0

        lax.fori_loop(1, nz, give, 0)
        for d in range(1, nx):
            remote(lost.at[x], lost.at[x], s3, r3, d, {"x": lax.rem(x + d, nx)}).start()
        got[pl.ds(z, 1)] = mine[...][None]

    beside_copy = remote(got, beside, s0, r0, 1, sibling)

    def spread():
        def done(d, _):
            p = lax.rem(z + nz - d, nz)
            remote(got.at[p], got.at[p], s2, r2, d, {"z": p}).wait_recv()
            return 0

        lax.fori_loop(1, nz, done, 0)
        beside_copy.start()

    def weigh(core, logs, first, count):
        def one(k, _):
            w = k * nc + core
            both = 0.0
            for i in range(2):
                level = stats[core, k, i, 0, :, pl.ds(0, rows)]
                share = jnp.exp2(level - logs[k, i, :, pl.ds(0, rows)])
                mass = masses[2 * w + i, :, :, pl.ds(0, rows)] * share[None]
                mass = mass.reshape(mass.shape[0] * mass.shape[1], rows).astype(jnp.bfloat16)
                both = both + jnp.dot(
                    mass, everyone[w, i * rows:(i + 1) * rows], preferred_element_type=jnp.float32
                )
            terms[w] = both
            return 0

        lax.fori_loop(first, first + count, one, 0)

    def cluster_copy(k):
        px, py = place(*pairs[k])
        return remote(cluster.at[py, px], parts.at[k], cl_s, cl_r, k, {"x": px, "y": py})

    def clusters():
        flat = terms[...].reshape(terms.shape[0] * terms.shape[1], width)
        pick = lax.broadcasted_iota(jnp.int32, (ny * per, flat.shape[0]), 0) == names[...]
        summed = jnp.dot(
            pick.astype(jnp.float32), flat, precision=lax.Precision.HIGHEST,
            preferred_element_type=jnp.float32,
        )
        for py in range(ny):
            for px in range(nx):
                cluster[py, px] = summed[py * per:(py + 1) * per, px * depth:(px + 1) * depth]
        for k in range(len(pairs)):
            cluster_copy(k).start()

    part = nz // 2
    tasks = [
        (0, send_stats),
        (2, total),
        (4, spread),
        (4, lambda: weigh(c, got, 0, part)),
        (5, lambda: weigh(c, got, part, nz - part)),
        (6, beside_copy.wait_recv),
        (6, lambda: weigh(1 - c, beside, 0, part)),
        (7, lambda: weigh(1 - c, beside, part, nz - part)),
        (7, clusters),
    ]

    begin(range(min(3, nz)))
    for levels in (klong_out, kshort_out):
        levels[...] = jnp.zeros_like(levels)
    over.wait_recv()
    for s in range(steps):
        ready(steps - s)
        if s > 0:
            ready(s - steps)
        for i in range(2):
            sign = 1 if i == 0 else -1
            extra = []
            if s > 0:
                arrive(longs(s - 1, i))
                extra = [(klong_in[s - 1, i, :, 0:rows], long_in[s - 1, i])]
            value, top = merged(sign * (steps - s) if s > 0 else steps, i, extra)
            long_out[s, i] = value.astype(jnp.bfloat16)
            klong_out[s, i, :, 0:rows] = top
            for copy in longs(s, i):
                copy.start()
            if s > 0:
                extra = []
                if s > 1:
                    arrive(shorts(s - 1, i))
                    extra = [(kshort_in[s - 2, i, :, 0:rows], short_in[s - 2, i])]
                value, top = merged(sign * (s - steps), i, extra)
                short_out[s - 1, i] = value.astype(jnp.bfloat16)
                kshort_out[s - 1, i, :, 0:rows] = top
                for copy in shorts(s, i):
                    copy.start()
        while tasks and (tasks[0][0] == s or s == steps - 1):
            tasks.pop(0)[1]()
    ready(0)
    for i in range(2):
        arrive(shorts(steps - 1, i))
        arrive(longs(steps - 1, i))
        value, top = merged(
            0, i,
            [
                (klong_in[steps - 1, i, :, 0:rows], long_in[steps - 1, i]),
                (kshort_in[steps - 2, i, :, 0:rows], short_in[steps - 2, i]),
            ],
        )
        wide = positive[i * rows:(i + 1) * rows].astype(jnp.float32)
        value = value * as_column(jnp.exp2(top - mine[i, :, 0:rows]))
        value = (value + as_column(factor[i, :, 0:rows]) * wide) * factor_scale
        for k in range(nx):
            final[k, i * rows:(i + 1) * rows] = value[:, k * depth:(k + 1) * depth]
    ends = []
    for d in range(1, nx):
        px = lax.rem(x + d, nx)
        copy = remote(final.at[px], landed.at[x], fin_s, fin_r, d, {"x": px})
        copy.start()
        ends.append(copy)
    whole = cluster[y, x]
    for k in range(len(pairs)):
        cluster_copy(k).wait_recv()
        whole = whole + parts[k]
    centroid_grad[...] = whole * factor_scale
    user_grad[pl.ds(x, 1)] = final[pl.ds(x, 1)]
    for d in range(1, nx):
        frm = lax.rem(x - d + nx, nx)
        remote(lost.at[frm], lost.at[frm], s3, r3, d, {"x": frm}).wait_recv()
    losses[...] = lost[...]
    for d in range(1, nx):
        frm = lax.rem(x - d + nx, nx)
        remote(landed.at[frm], landed.at[frm], fin_s, fin_r, d, {"x": frm}).wait_recv()
        user_grad[pl.ds(frm, 1)] = landed[pl.ds(frm, 1)]

    for copy in crossing + [cluster_copy(k) for k in range(len(pairs))] + ends + [over, beside_copy]:
        copy.wait_send()
    for i in range(2):
        for s in range(steps):
            for copy in longs(s, i) + (shorts(s, i) if s > 0 else ()):
                copy.wait_send()

    def left(d, _):
        p = lax.rem(z + d, nz)
        remote(joined.at[p], came.at[z], s1, r1, d, {"z": p}).wait_send()
        remote(mine, got.at[z], s2, r2, d, {"z": p}).wait_send()
        return 0

    lax.fori_loop(1, nz, left, 0)
    for d in range(1, nx):
        remote(lost.at[x], lost.at[x], s3, r3, d, {"x": lax.rem(x + d, nx)}).wait_send()


def params(identity=None, megabytes=48):
    return pltpu.CompilerParams(
        collective_id=identity,
        has_side_effects=identity is not None,
        vmem_limit_bytes=megabytes * 1024 * 1024,
    )


def lanes_of(rows):
    return -(-rows // 128) * 128


def buffers_of(rows, width, nx, quarter):
    return [
        pltpu.VMEM((SLOTS, rows, width), jnp.bfloat16),
        pltpu.VMEM((SLOTS, nx, quarter, width), jnp.bfloat16),
        pltpu.SemaphoreType.DMA((SLOTS,)),
        pltpu.SemaphoreType.DMA((SLOTS,)),
    ]


def flash_call(nw, ny, half, scale, rows, width, nx, quarter):
    sds = jax.ShapeDtypeStruct
    lanes = lanes_of(rows)
    return pl.pallas_call(
        functools.partial(flash_kernel, half, scale),
        out_shape=(
            sds((2, nw // 2, 2, 2, 1, lanes), jnp.float32),
            sds((2 * nw, ny, MASS_ROWS, lanes), jnp.float32),
            sds((2 * nw, rows, width), jnp.bfloat16),
        ),
        in_specs=[SMEM, SMEM, HBM, HBM, VMEM, HBM],
        out_specs=[VMEM, VMEM, HBM],
        input_output_aliases={5: 2},
        scratch_shapes=[pltpu.SMEM((2, nw * ny + 8), jnp.int32)]
        + buffers_of(rows, width, nx, quarter)
        + [
            pltpu.VMEM((rows, width), jnp.float32),
            pltpu.VMEM((2, rows, width), jnp.bfloat16),
            pltpu.SemaphoreType.DMA((2,)),
        ],
        compiler_params=params(None, 58),
        name="flash",
    )


def return_call(sizes, scale, rows, width, per):
    nx, nz, ny, nc = sizes
    lanes, depth, steps, nw = lanes_of(rows), width // nx, nz // 2, nz * nc
    sds = lambda *shape: jax.ShapeDtypeStruct(shape, jnp.float32)
    buffer = lambda *shape: pltpu.VMEM(shape, jnp.float32)
    ring = lambda n: pltpu.VMEM((n, 2, rows, width), jnp.bfloat16)
    dma = pltpu.SemaphoreType.DMA
    return pl.pallas_call(
        functools.partial(return_kernel, sizes, scale, LOSS_SCALE * scale),
        out_shape=(sds(nx, 2 * rows, depth), sds(per, depth), sds(nx, 2, 1, lanes)),
        in_specs=[HBM, VMEM, VMEM, VMEM, HBM, VMEM],
        out_specs=[VMEM] * 3,
        scratch_shapes=[
            ring(nz), ring(nz), ring(steps), ring(steps), ring(steps - 1), ring(steps - 1),
            buffer(steps, 2, 1, lanes), buffer(steps, 2, 1, lanes),
            buffer(steps - 1, 2, 1, lanes), buffer(steps - 1, 2, 1, lanes),
            buffer(nx, 2 * rows, depth), buffer(nx, 2 * rows, depth),
            buffer(max(nx * ny - 1, 1), per, depth), buffer(ny, nx, per, depth),
            pltpu.VMEM((nw, 2 * rows, width), jnp.bfloat16),
            buffer(nw, ny * MASS_ROWS, width),
            buffer(nz, 2, 2, 1, lanes), buffer(nz, 2, 2, 1, lanes), buffer(nz, 2, 2, 1, lanes),
            buffer(2, 1, lanes), buffer(nz, 2, 1, lanes), buffer(nz, 2, 1, lanes),
            buffer(nx, 2, 1, lanes), buffer(2, 1, lanes),
            dma((nz,)), dma((nz,)), dma((nz,)),
        ]
        + [dma((2 * steps,))] * 8
        + [dma((nx,))] * 2
        + [dma((nx * ny,))] * 2
        + [dma((2,))] * 2
        + [dma((nz,))] * 4
        + [dma((nx,))] * 2
        + [dma((1,))],
        compiler_params=params(2, 58),
        name="return",
    )


def local(
    sizes, user_rows, positive_rows, centroids, residuals, block_lists, block_lengths,
    cluster_counts, ad_counts,
):
    nx, nz, ny, nc = sizes
    x, z, y, c = (lax.axis_index(a) for a in AXES)
    nw, shards = nz * nc, nz * ny * nc
    per, width = centroids.shape
    quarter = residuals.shape[1]
    tile = ad_counts.shape[1]
    blocks, listed = block_lists.shape
    rows = user_rows.shape[0] // blocks
    half = per // 2
    scale = 1.0 / math.sqrt(width)
    sds = jax.ShapeDtypeStruct
    dma = pltpu.SemaphoreType.DMA
    bf16, f32 = jnp.bfloat16, jnp.float32

    ad_rows = (centroids[:, None, :] + residuals.astype(f32)).astype(bf16)
    weights = ad_counts.astype(f32)
    expected = (
        cluster_counts.astype(f32)[:, None] * weights / jnp.sum(weights, axis=1, keepdims=True)
    )
    shift = jnp.log(expected).astype(bf16)
    flat = block_lists.reshape(blocks * listed)
    used = jnp.arange(listed)[None, :] < block_lengths[:, None]
    name = jnp.where(used, jnp.arange(blocks)[:, None] + 1, 0).reshape(blocks * listed)
    match = flat[:, None] // per == jnp.arange(shards)[None, :]
    block_of = jnp.sum(jnp.where(match, name[:, None], 0), axis=0) - 1
    place_of = jnp.sum(jnp.where(match, (flat % per)[:, None], 0), axis=0)
    codes = jnp.stack([block_of, place_of]).astype(f32).astype(bf16)
    codes = jnp.pad(codes, ((0, CODE_ROWS - 2), (0, width - shards)))

    steps = nz // 2
    copies = 2 * (nx - 1) + (ny - 1) + 8 + 4 + 12 + 16 + (nz - 1) + nz
    mine = 2 * rows
    all_tiles, all_users, positives, all_shift, zeroed = pl.pallas_call(
        functools.partial(gather_kernel, sizes),
        out_shape=(
            sds((ny, nx, 2, half, quarter, width), bf16),
            sds((nz, nc, mine + CODE_ROWS, width), bf16),
            sds((mine, width), bf16),
            sds((ny, per, tile), bf16),
            sds((2 * nw, rows, width), bf16),
        ),
        in_specs=[HBM] * 5,
        out_specs=[HBM] * 5,
        scratch_shapes=[
            dma((copies,)), dma((copies,)), dma((5,)),
            pltpu.VMEM((4, rows, width), bf16), dma((nw // 2,)),
        ],
        compiler_params=params(0, 58),
        name="gather",
    )(ad_rows.reshape(2, half, quarter, width), user_rows, positive_rows, codes, shift)

    picked = all_users[:, :, mine:mine + 2, :shards].reshape(nw, 2, nz, ny, nc)
    picked = lax.dynamic_index_in_dim(picked, z, 2, keepdims=False)
    picked = lax.dynamic_index_in_dim(picked, c, 3, keepdims=False)
    places = jnp.swapaxes(picked, 0, 1).reshape(2, nw * ny).astype(jnp.int32)
    flat_users = all_users.reshape(nw, mine + CODE_ROWS, width)
    flat_shift = all_shift.reshape(ny * per, tile)
    stats, masses, grads = flash_call(nw, ny, half, scale, rows, width, nx, quarter)(
        places, x.astype(jnp.int32).reshape(1), flat_users, all_tiles, flat_shift, zeroed
    )
    depth = width // nx
    names = places[1].reshape(nw, ny) + per * jnp.arange(ny)[None, :]
    names = jnp.repeat(names.reshape(1, nw * ny), MASS_ROWS, axis=1)
    user_grad, centroid_grad, losses = return_call(sizes, scale, rows, width, per)(
        grads.reshape(nz, nc, 2, rows, width), stats, masses, names, flat_users, positives
    )
    return (
        losses[:, :, 0, :rows].reshape(blocks * rows),
        user_grad.reshape(blocks * rows, depth),
        centroid_grad,
    )


def build(mesh, sizes):
    return jax.shard_map(
        functools.partial(local, sizes),
        mesh=mesh,
        in_specs=(
            P(("z", "y", "c"), "x"),
            P(("z", "y", "c"), "x"),
            P(("z", "y", "c"), None),
            P(("z", "y", "c"), "x", None),
            P(("z", "y", "c"), None),
            P(("z", "y", "c")),
            P(("z", "y", "c")),
            P(("z", "y", "c"), None),
        ),
        out_specs=(P(("z", "y", "c")), P(("z", "y", "c"), "x"), P(("z", "y", "c"), "x")),
        check_vma=False,
    )


def solution(mesh):
    sizes = (mesh.shape["tower"],) + SPLIT
    return build(Mesh(mesh.devices.reshape(sizes), AXES), sizes)
```

time: 357 us -> 335 us (0.938)
  Pallas kernels: 335 us -> 315 us
    pallas_call x4 -> x2, Pallas kernels: 143 us -> 122 us  [the longest x1 107 us: local(): return_call(sizes, scale, rows, width, per)]
where the time goes in v3:
time: 335 us; the launch traced here: 334 us
  Pallas kernels  315 us (94%)
  local copies, waits for them, and re-layouts  11.3 us (3%)
  other arithmetic  7.5 us (2%)
    pallas_call x1, Pallas kernels, local(): pl.pallas_call(functools.partial(gather_kernel, sizes), out_shape=(sds((n...  192 us
    pallas_call x1, Pallas kernels, local(): return_call(sizes, scale, rows, width, per)  107 us
    pallas_call x1, Pallas kernels, local(): flash_call(nw, ny, half, scale, rows, width, nx, quarter)  15.6 us

profile of v3, /device:TPU:1, one launch (start us, length us, event | category | flops | bytes accessed | tf_op | source)
XLA Modules:
  0.0 334.2 jit_solution(2950439188615763023)
XLA Ops:
  0.6 0.8 broadcast_in_dim_reshape.4
  1.4 0.7 convert_element_type.36
  2.1 0.9 convert_reduce_fusion
  3.0 0.7 fusion
  3.7 0.1 select_n.53
  3.8 0.1 select_reduce_fusion.1
  3.9 1.5 log_convert_fusion.shift
  5.4 0.6 pad.4.codes
  6.0 0.1 add.74
  6.1 3.5 %add_convert_fusion = bf16[32,64,512]{2,1,0:T(8,128)(2,1)} fusion(bf16[32,64,512]{2,1,0:T(8,128)(2,1)} %param.11, f32[32,512]{1,0:T(8,128)} %param.10), kind=kLoop, calls=%fused_computation | loop fusion | flops 3145728 | bytes 4259840 | tf_op jit(solution)/shard_map/convert_element_type | solution.py:742
  9.6 192.4 %gather.1 = (bf16[4,4,2,16,64,512]{5,4,3,2,1,0:T(8,128)(2,1)}, bf16[16,2,400,512]{3,2,1,0:T(8,128)(2,1)}, bf16[384,512]{1,0:T(8,128)(2,1)}, bf16[4,32,256]{2,1,0:T(8,128)(2,1)}, bf16[64,192,512]{2,1,0:T(8,128)(2,1)}) custom-call(bf16[2,16,64,512]{3,2,1,0:T(8,128)(2,1)} %bitcast.17, bf16[1536,128]{1,0:T(8,128)(2,1)} %users.1, bf16[1536,128]{1,0:T(8,128)(2,1)} %positives.1, ...), custom_call_target="tpu_custom_call" | custom-call | tf_op jit(solution)/shard_map/gather/pallas_call | solution.py:760
  202.1 0.9 slice.12
  202.9 2.2 reshape.181
  205.2 0.1 dynamic-slice_convert_fusion
  205.3 0.1 copy.21
  205.4 0.1 copy.18
  205.5 0.1 slice.14
  205.6 0.1 copy.17
  205.7 0.7 convert_element_type.42.codes
  206.4 15.6 %flash.1 = (f32[2,16,2,2,1,256]{5,4,3,2,1,0:T(1,128)}, f32[64,4,8,256]{3,2,1,0:T(8,128)}, bf16[64,192,512]{2,1,0:T(8,128)(2,1)}) custom-call(s32[2,128]{1,0:T(2,128)} %convert_element_type.42.codes, s32[1]{0:T(128)} %bitcast.5.mine, bf16[32,400,512]{2,1,0:T(8,128)(2,1)} %bitcast.14, ...), custom_call_target="tpu_custom_call", output_to_operand_aliasing={{2}: (5, {})} | custom-call | tf_op jit(solution)/shard_map/flash/pallas_call | solution.py:785
  222.0 0.1 broadcast_in_dim.46
  222.0 0.7 broadcast_in_dim.47.names
  222.8 106.6 %return.1 = (f32[4,384,128]{2,1,0:T(8,128)}, f32[32,128]{1,0:T(8,128)}, f32[4,2,1,256]{3,2,1,0:T(1,128)}) custom-call(bf16[16,2,2,192,512]{4,3,2,1,0:T(8,128)(2,1)} %bitcast.16, f32[2,16,2,2,1,256]{5,4,3,2,1,0:T(1,128)} %get-tuple-element.19.stats, f32[64,4,8,256]{3,2,1,0:T(8,128)} %get-tuple-element.20.masses, s32[1,1024]{1,0:T(1,128)} %broadcast_in_dim.47.names, ...), custom_call_target="tpu_custom_call" | custom-call | tf_op jit(solution)/shard_map/return/pallas_call | solution.py:791
  329.4 0.7 slice_reduce_fusion
  330.1 0.7 reshape_squeeze.4
  330.8 2.1 copy.25
  332.8 1.3 copy.26
  (8 shorter events, 0.0 us)

commit v4 on v3

--- a/solution.py
+++ b/solution.py
@@ -42,8 +42,8 @@
 
 
 def gather_kernel(
-    sizes, tiles, users, positives, codes, shift,
-    all_tiles, all_users, own_positives, all_shift, zeroed, sends, recvs, locals_, zbuf, zsem,
+    sizes, tiles, users, codes, shift,
+    all_tiles, all_users, all_shift, zeroed, sends, recvs, locals_, zbuf, zsem,
 ):
     nx, nz, ny, nc = sizes
     x, z, y, c = (lax.axis_index(a) for a in AXES)
@@ -104,7 +104,6 @@
         pltpu.make_async_copy(codes, home.at[pl.ds(rows, CODE_ROWS)], locals_.at[1]),
         pltpu.make_async_copy(tiles, all_tiles.at[y, x], locals_.at[2]),
         pltpu.make_async_copy(shift, all_shift.at[y], locals_.at[3]),
-        pltpu.make_async_copy(positives.at[part(x)], own_positives.at[:, columns(x)], locals_.at[4]),
     ]
     for copy in own:
         copy.start()
@@ -121,13 +120,6 @@
     for h in (0, 1):
         for d in (1, -1):
             p2[h, 0, d] = push(tiles.at[h], block(h, 0, 0), second[h](d), block(h, 0, -d))
-    for d in range(1, nx):
-        late.append(
-            push(
-                positives.at[part(at_x(d))], own_positives.at[:, columns(x)], to_x(d),
-                own_positives.at[:, columns(at_x(-d))],
-            )
-        )
     for d in range(1, ny):
         late.append(push(shift, all_shift.at[y], to_y(d), all_shift.at[at_y(-d)]))
 
@@ -253,8 +245,8 @@
         for i in range(2):
             for yp in range(ny):
                 list_ref[0, n] = w * 2 + i
-                list_ref[1, n] = yp * (2 * half) + codes[1, w * ny + yp]
-                n = n + (codes[0, w * ny + yp] == 2 * t + i).astype(jnp.int32)
+                list_ref[1, n] = yp * (2 * half) + codes[2 * w + 1, yp]
+                n = n + (codes[2 * w, yp] == 2 * t + i).astype(jnp.int32)
         return n
 
     total = lax.fori_loop(0, nw, gather, jnp.int32(0))
@@ -355,15 +347,15 @@
 
 
 def return_kernel(
-    sizes, scale, factor_scale, grads, stats, masses, names, users, positive,
+    sizes, scale, factor_scale, grads, stats, masses, names, users, positives,
     user_grad, centroid_grad, losses,
     own, sib, long_out, long_in, short_out, short_in,
     klong_out, klong_in, kshort_out, kshort_in,
     final, landed, parts, cluster, everyone, terms,
-    across, joined, came, mine, got, beside, lost, factor,
+    across, joined, came, mine, got, beside, lost, factor, positive,
     own_sem, sib_s, sib_r, long_s, long_r, short_s, short_r,
     kl_s, kl_r, ks_s, ks_r, fin_s, fin_r, cl_s, cl_r,
-    s0, r0, s1, r1, s2, r2, s3, r3, usem,
+    s0, r0, s1, r1, s2, r2, s3, r3, s4, r4, usem,
 ):
     nx, nz, ny, nc = sizes
     x, z, y, c = (lax.axis_index(a) for a in AXES)
@@ -438,9 +430,20 @@
         for copy in copies:
             copy.wait_recv()
 
+    part_of = lambda i: pl.ds(pl.multiple_of(i * 2 * rows, 2 * rows), 2 * rows)
+    columns = lambda i: pl.ds(pl.multiple_of(i * depth, depth), depth)
+    own_part = pltpu.make_async_copy(positives.at[part_of(x)], positive.at[:, columns(x)], usem.at[1])
+
+    def positive_copy(d):
+        px = lax.rem(x + d, nx)
+        return remote(positives.at[part_of(px)], positive.at[:, columns(x)], s4, r4, d, {"x": px})
+
     def send_stats():
         begin(range(min(3, nz), nz))
         pltpu.make_async_copy(users.at[:, pl.ds(0, 2 * rows)], everyone, usem.at[0]).start()
+        own_part.start()
+        for d in range(1, nx):
+            positive_copy(d).start()
         here = stats[pl.ds(c, 1)][0]
         there = across[...]
         tops = jnp.maximum(here[:, :, 0], there[:, :, 0])
@@ -462,6 +465,11 @@
 
     def total():
         pltpu.make_async_copy(users.at[:, pl.ds(0, 2 * rows)], everyone, usem.at[0]).wait()
+        own_part.wait()
+        for d in range(1, nx):
+            frm = lax.rem(x - d + nx, nx)
+            landing = positive.at[:, columns(frm)]
+            remote(landing, landing, s4, r4, d, {"x": frm}).wait_recv()
 
         def come(d, _):
             p = lax.rem(z + nz - d, nz)
@@ -583,6 +591,10 @@
                     copy.start()
         while tasks and (tasks[0][0] == s or s == steps - 1):
             tasks.pop(0)[1]()
+    def end(d, i):
+        px = lax.rem(x + d, nx)
+        return remote(final.at[px, i], landed.at[x, i], fin_s, fin_r, 2 * d + i, {"x": px})
+
     ready(0)
     for i in range(2):
         arrive(shorts(steps - 1, i))
@@ -598,13 +610,9 @@
         value = value * as_column(jnp.exp2(top - mine[i, :, 0:rows]))
         value = (value + as_column(factor[i, :, 0:rows]) * wide) * factor_scale
         for k in range(nx):
-            final[k, i * rows:(i + 1) * rows] = value[:, k * depth:(k + 1) * depth]
-    ends = []
-    for d in range(1, nx):
-        px = lax.rem(x + d, nx)
-        copy = remote(final.at[px], landed.at[x], fin_s, fin_r, d, {"x": px})
-        copy.start()
-        ends.append(copy)
+            final[k, i] = value[:, k * depth:(k + 1) * depth]
+        for d in range(1, nx):
+            end(d, i).start()
     whole = cluster[y, x]
     for k in range(len(pairs)):
         cluster_copy(k).wait_recv()
@@ -615,17 +623,21 @@
         frm = lax.rem(x - d + nx, nx)
         remote(lost.at[frm], lost.at[frm], s3, r3, d, {"x": frm}).wait_recv()
     losses[...] = lost[...]
-    for d in range(1, nx):
-        frm = lax.rem(x - d + nx, nx)
-        remote(landed.at[frm], landed.at[frm], fin_s, fin_r, d, {"x": frm}).wait_recv()
-        user_grad[pl.ds(frm, 1)] = landed[pl.ds(frm, 1)]
-
-    for copy in crossing + [cluster_copy(k) for k in range(len(pairs))] + ends + [over, beside_copy]:
+    for i in range(2):
+        for d in range(1, nx):
+            frm = lax.rem(x - d + nx, nx)
+            landing = landed.at[frm, i]
+            remote(landing, landing, fin_s, fin_r, 2 * d + i, {"x": frm}).wait_recv()
+            user_grad[pl.ds(frm, 1), i] = landed[pl.ds(frm, 1), i]
+
+    for copy in crossing + [cluster_copy(k) for k in range(len(pairs))] + [over, beside_copy]:
         copy.wait_send()
     for i in range(2):
         for s in range(steps):
             for copy in longs(s, i) + (shorts(s, i) if s > 0 else ()):
                 copy.wait_send()
+        for d in range(1, nx):
+            end(d, i).wait_send()
 
     def left(d, _):
         p = lax.rem(z + d, nz)
@@ -636,6 +648,7 @@
     lax.fori_loop(1, nz, left, 0)
     for d in range(1, nx):
         remote(lost.at[x], lost.at[x], s3, r3, d, {"x": lax.rem(x + d, nx)}).wait_send()
+        positive_copy(d).wait_send()
 
 
 def params(identity=None, megabytes=48):
@@ -693,29 +706,30 @@
     dma = pltpu.SemaphoreType.DMA
     return pl.pallas_call(
         functools.partial(return_kernel, sizes, scale, LOSS_SCALE * scale),
-        out_shape=(sds(nx, 2 * rows, depth), sds(per, depth), sds(nx, 2, 1, lanes)),
-        in_specs=[HBM, VMEM, VMEM, VMEM, HBM, VMEM],
+        out_shape=(sds(nx, 2, rows, depth), sds(per, depth), sds(nx, 2, 1, lanes)),
+        in_specs=[HBM, VMEM, VMEM, VMEM, HBM, HBM],
         out_specs=[VMEM] * 3,
         scratch_shapes=[
             ring(nz), ring(nz), ring(steps), ring(steps), ring(steps - 1), ring(steps - 1),
             buffer(steps, 2, 1, lanes), buffer(steps, 2, 1, lanes),
             buffer(steps - 1, 2, 1, lanes), buffer(steps - 1, 2, 1, lanes),
-            buffer(nx, 2 * rows, depth), buffer(nx, 2 * rows, depth),
+            buffer(nx, 2, rows, depth), buffer(nx, 2, rows, depth),
             buffer(max(nx * ny - 1, 1), per, depth), buffer(ny, nx, per, depth),
             pltpu.VMEM((nw, 2 * rows, width), jnp.bfloat16),
             buffer(nw, ny * MASS_ROWS, width),
             buffer(nz, 2, 2, 1, lanes), buffer(nz, 2, 2, 1, lanes), buffer(nz, 2, 2, 1, lanes),
             buffer(2, 1, lanes), buffer(nz, 2, 1, lanes), buffer(nz, 2, 1, lanes),
             buffer(nx, 2, 1, lanes), buffer(2, 1, lanes),
+            pltpu.VMEM((2 * rows, width), jnp.bfloat16),
             dma((nz,)), dma((nz,)), dma((nz,)),
         ]
         + [dma((2 * steps,))] * 8
-        + [dma((nx,))] * 2
+        + [dma((2 * nx,))] * 2
         + [dma((nx * ny,))] * 2
         + [dma((2,))] * 2
         + [dma((nz,))] * 4
-        + [dma((nx,))] * 2
-        + [dma((1,))],
+        + [dma((nx,))] * 4
+        + [dma((2,))],
         compiler_params=params(2, 58),
         name="return",
     )
@@ -755,41 +769,39 @@
     codes = jnp.pad(codes, ((0, CODE_ROWS - 2), (0, width - shards)))
 
     steps = nz // 2
-    copies = 2 * (nx - 1) + (ny - 1) + 8 + 4 + 12 + 16 + (nz - 1) + nz
+    copies = (nx - 1) + (ny - 1) + 8 + 4 + 12 + 16 + (nz - 1) + nz
     mine = 2 * rows
-    all_tiles, all_users, positives, all_shift, zeroed = pl.pallas_call(
+    all_tiles, all_users, all_shift, zeroed = pl.pallas_call(
         functools.partial(gather_kernel, sizes),
         out_shape=(
             sds((ny, nx, 2, half, quarter, width), bf16),
             sds((nz, nc, mine + CODE_ROWS, width), bf16),
-            sds((mine, width), bf16),
             sds((ny, per, tile), bf16),
             sds((2 * nw, rows, width), bf16),
         ),
-        in_specs=[HBM] * 5,
-        out_specs=[HBM] * 5,
+        in_specs=[HBM] * 4,
+        out_specs=[HBM] * 4,
         scratch_shapes=[
-            dma((copies,)), dma((copies,)), dma((5,)),
+            dma((copies,)), dma((copies,)), dma((4,)),
             pltpu.VMEM((4, rows, width), bf16), dma((nw // 2,)),
         ],
         compiler_params=params(0, 58),
         name="gather",
-    )(ad_rows.reshape(2, half, quarter, width), user_rows, positive_rows, codes, shift)
-
-    picked = all_users[:, :, mine:mine + 2, :shards].reshape(nw, 2, nz, ny, nc)
-    picked = lax.dynamic_index_in_dim(picked, z, 2, keepdims=False)
-    picked = lax.dynamic_index_in_dim(picked, c, 3, keepdims=False)
-    places = jnp.swapaxes(picked, 0, 1).reshape(2, nw * ny).astype(jnp.int32)
+    )(ad_rows.reshape(2, half, quarter, width), user_rows, codes, shift)
+
+    pick = jnp.arange(shards)[:, None] == z * ny * nc + jnp.arange(ny)[None, :] * nc + c
+    found = all_users[:, :, mine:mine + 2, :shards].reshape(nw * 2, shards)
+    places = jnp.dot(found, pick.astype(bf16), preferred_element_type=f32).astype(jnp.int32)
     flat_users = all_users.reshape(nw, mine + CODE_ROWS, width)
     flat_shift = all_shift.reshape(ny * per, tile)
     stats, masses, grads = flash_call(nw, ny, half, scale, rows, width, nx, quarter)(
         places, x.astype(jnp.int32).reshape(1), flat_users, all_tiles, flat_shift, zeroed
     )
     depth = width // nx
-    names = places[1].reshape(nw, ny) + per * jnp.arange(ny)[None, :]
+    names = places.reshape(nw, 2, ny)[:, 1] + per * jnp.arange(ny)[None, :]
     names = jnp.repeat(names.reshape(1, nw * ny), MASS_ROWS, axis=1)
     user_grad, centroid_grad, losses = return_call(sizes, scale, rows, width, per)(
-        grads.reshape(nz, nc, 2, rows, width), stats, masses, names, flat_users, positives
+        grads.reshape(nz, nc, 2, rows, width), stats, masses, names, flat_users, positive_rows
     )
     return (
         losses[:, :, 0, :rows].reshape(blocks * rows),

time: 335 us -> 322 us (0.961)
  Pallas kernels: 315 us -> 305 us
    pallas_call x1, Pallas kernels: 107 us -> 96.8 us  [local(): return_call(sizes, scale, rows, width, per)]
    pallas_call x1, Pallas kernels: 15.6 us -> 20.5 us  [local(): flash_call(nw, ny, half, scale, rows, width, nx, quarter)]
    pallas_call x1, Pallas kernels: 192 us -> 188 us  [local(): pl.pallas_call(functools.partial(gather_kernel, sizes), out_shape=(sds((n...]
where the time goes in v4:
time: 322 us; the launch traced here: 320 us
  Pallas kernels  305 us (95%)
  local copies, waits for them, and re-layouts  8.13 us (3%)
  other arithmetic  5.22 us (2%)
    pallas_call x1, Pallas kernels, local(): pl.pallas_call(functools.partial(gather_kernel, sizes), out_shape=(sds((n...  188 us
    pallas_call x1, Pallas kernels, local(): return_call(sizes, scale, rows, width, per)  96.8 us
    pallas_call x1, Pallas kernels, local(): flash_call(nw, ny, half, scale, rows, width, nx, quarter)  20.5 us

profile of v4, /device:TPU:1, one launch (start us, length us, event | category | flops | bytes accessed | tf_op | source)
XLA Modules:
  0.0 320.3 jit_solution(14050154309518136045)
XLA Ops:
  0.6 0.0 copy-start.2
  0.6 0.0 copy-start.1
  0.7 0.8 broadcast_in_dim_reshape.4
  1.5 0.7 fusion.1
  2.2 0.1 select_n.41
  2.3 0.1 select_reduce_fusion.1
  2.4 0.6 pad.4.codes
  3.0 3.5 %add_convert_fusion = bf16[32,64,512]{2,1,0:T(8,128)(2,1)} fusion(bf16[32,64,512]{2,1,0:T(8,128)(2,1)} %param.11, f32[32,512]{1,0:T(8,128)} %param.10), kind=kLoop, calls=%fused_computation | loop fusion | flops 3145728 | bytes 4259840 | tf_op jit(solution)/shard_map/convert_element_type | solution.py:756
  6.5 0.0 copy-done.2
  6.5 0.0 copy-done.1
  6.5 0.1 convert_reduce_fusion
  6.7 0.7 log_convert_fusion.shift
  7.4 188.2 %gather.1 = (bf16[4,4,2,16,64,512]{5,4,3,2,1,0:T(8,128)(2,1)}, bf16[16,2,400,512]{3,2,1,0:T(8,128)(2,1)}, bf16[4,32,256]{2,1,0:T(8,128)(2,1)}, bf16[64,192,512]{2,1,0:T(8,128)(2,1)}) custom-call(bf16[2,16,64,512]{3,2,1,0:T(8,128)(2,1)} %bitcast.18, bf16[1536,128]{1,0:T(8,128)(2,1)} %users.1, bf16[16,512]{1,0:T(8,128)(2,1)} %pad.4.codes, ...), custom_call_target="tpu_custom_call" | custom-call | tf_op jit(solution)/shard_map/gather/pallas_call | solution.py:774
  195.5 0.9 slice.9
  196.4 0.7 convolution_convert_fusion.codes
  197.1 0.0 copy-start
  197.1 20.5 %flash.1 = (f32[2,16,2,2,1,256]{5,4,3,2,1,0:T(1,128)}, f32[64,4,8,256]{3,2,1,0:T(8,128)}, bf16[64,192,512]{2,1,0:T(8,128)(2,1)}) custom-call(s32[64,4]{1,0:T(8,128)} %convolution_convert_fusion.codes, s32[1]{0:T(128)} %bitcast.4.mine, bf16[32,400,512]{2,1,0:T(8,128)(2,1)} %bitcast.15, ...), custom_call_target="tpu_custom_call", output_to_operand_aliasing={{2}: (5, {})} | custom-call | tf_op jit(solution)/shard_map/flash/pallas_call | solution.py:797
  217.6 0.0 copy-done
  217.7 0.1 squeeze.3
  217.8 0.1 add.86
  217.9 0.1 broadcast_in_dim.48
  218.0 0.7 broadcast_in_dim.49.names
  218.7 96.8 %return.1 = (f32[4,2,192,128]{3,2,1,0:T(8,128)}, f32[32,128]{1,0:T(8,128)}, f32[4,2,1,256]{3,2,1,0:T(1,128)}) custom-call(bf16[16,2,2,192,512]{4,3,2,1,0:T(8,128)(2,1)} %bitcast.17, f32[2,16,2,2,1,256]{5,4,3,2,1,0:T(1,128)} %get-tuple-element.18.stats, f32[64,4,8,256]{3,2,1,0:T(8,128)} %get-tuple-element.19.masses, s32[1,1024]{1,0:T(1,128)} %broadcast_in_dim.49.names, ...), custom_call_target="tpu_custom_call" | custom-call | tf_op jit(solution)/shard_map/return/pallas_call | solution.py:803
  315.5 0.7 slice_reduce_fusion
  316.2 0.7 reshape_squeeze.3
  316.9 2.1 copy.23
  319.0 1.3 copy.24
  (10 shorter events, 0.1 us)
Async XLA Ops:
  0.6 5.9 %copy-start.2 = (s32[32]{0:T(128)S(1)}, s32[32]{0:T(128)}, u32[]{:S(2)}) copy-start(s32[32]{0:T(128)} %param.14) | copy-start | bytes 388
  0.6 5.9 %copy-start.1 = (s32[32,256]{1,0:T(8,128)S(1)}, s32[32,256]{1,0:T(8,128)}, u32[]{:S(2)}) copy-start(s32[32,256]{1,0:T(8,128)} %param.15) | copy-start | bytes 98308
  197.1 20.5 %copy-start = (s32[64,4]{1,0:T(8,128)S(1)}, s32[64,4]{1,0:T(8,128)}, u32[]{:S(2)}) copy-start(s32[64,4]{1,0:T(8,128)} %convolution_convert_fusion.codes) | copy-start | bytes 3076

commit v5 on v4

--- a/solution.py
+++ b/solution.py
@@ -203,8 +203,8 @@
     assert count[0] == sends.shape[0], count[0]
 
 
-def fetch(users, tiles, list_ref, ubuf, tbuf, usem, tsem, half, e, slot):
-    b, tile = list_ref[0, e], list_ref[1, e]
+def fetch(users, tiles, entry, ubuf, tbuf, usem, tsem, half, e, slot):
+    b, tile = entry(e)
     per = 2 * half
     yp, cl = tile // per, tile % per
     w, i = b // 2, b % 2
@@ -219,16 +219,20 @@
     )
 
 
+def ads_of(tbuf, slot):
+    return tbuf[slot].reshape(tbuf.shape[1] * tbuf.shape[2], tbuf.shape[3])
+
+
 def scores(ubuf, tbuf, shift_ref, slot, tile, scale):
     user = ubuf[slot]
-    ads = tbuf[slot].reshape(tbuf.shape[1] * tbuf.shape[2], tbuf.shape[3])
+    ads = ads_of(tbuf, slot)
     pick = lax.broadcasted_iota(jnp.int32, (shift_ref.shape[0], user.shape[0]), 0) == tile
     shift = lax.dot_general(
         shift_ref[...], pick.astype(jnp.float32).astype(jnp.bfloat16), (((0,), (0,)), ((), ())),
         preferred_element_type=jnp.float32,
     )
     raw = lax.dot_general(ads, user, (((1,), (1,)), ((), ())), preferred_element_type=jnp.float32)
-    return user, ads, raw * scale - shift
+    return raw * scale - shift
 
 
 def flash_kernel(
@@ -240,19 +244,21 @@
     rows = ubuf.shape[1]
     parts = tbuf.shape[1]
     t = mine[0]
+    tiles_all = ny * 2 * half
+
+    def entry(e):
+        return list_ref[e] // tiles_all, list_ref[e] % tiles_all
 
     def gather(w, n):
         for i in range(2):
             for yp in range(ny):
-                list_ref[0, n] = w * 2 + i
-                list_ref[1, n] = yp * (2 * half) + codes[2 * w + 1, yp]
+                list_ref[n] = (w * 2 + i) * tiles_all + yp * (2 * half) + codes[2 * w + 1, yp]
                 n = n + (codes[2 * w, yp] == 2 * t + i).astype(jnp.int32)
         return n
 
     total = lax.fori_loop(0, nw, gather, jnp.int32(0))
-    list_ref[0, total] = -1
-    list_ref[1, total] = 0
-    get = functools.partial(fetch, users, tiles, list_ref, ubuf, tbuf, usem, tsem, half)
+    list_ref[total] = 2 * nw * tiles_all
+    get = functools.partial(fetch, users, tiles, entry, ubuf, tbuf, usem, tsem, half)
     ahead = ubuf.shape[0] - 1
     for k in range(ahead):
         @pl.when(total > k)
@@ -267,7 +273,16 @@
     def put(b, slot):
         return pltpu.make_async_copy(gout.at[slot], grads.at[b], gsem.at[slot])
 
-    def step(e, n):
+    def score(e):
+        return scores(ubuf, tbuf, shift_ref, e % (ahead + 1), entry(e)[1], scale)
+
+    @pl.when(total > 0)
+    def _():
+        for copy in get(0, 0):
+            copy.wait()
+
+    def step(e, held_over):
+        n, logits = held_over
         slot = e % (ahead + 1)
 
         @pl.when(e + ahead < total)
@@ -275,13 +290,17 @@
             for copy in get(e + ahead, (e + ahead) % (ahead + 1)):
                 copy.start()
 
-        for copy in get(e, slot):
-            copy.wait()
-        b, tile = list_ref[0, e], list_ref[1, e]
-        fresh = jnp.logical_or(e == 0, list_ref[0, jnp.maximum(e - 1, 0)] != b)
-        last = list_ref[0, e + 1] != b
+        @pl.when(e + 1 < total)
+        def _():
+            for copy in get(e + 1, (e + 1) % (ahead + 1)):
+                copy.wait()
+
+        b, tile = entry(e)
+        fresh = jnp.logical_or(e == 0, entry(jnp.maximum(e - 1, 0))[0] != b)
+        last = entry(e + 1)[0] != b
         at = ((b // 2) % 2, b // 4, b % 2)
-        user, ads, logits = scores(ubuf, tbuf, shift_ref, slot, tile, scale)
+        later = score(e + 1)
+        ads = ads_of(tbuf, slot)
         logits = logits * LOG2E
         before = stats[at + (0, slice(None), pl.ds(0, rows))]
         held = stats[at + (1, slice(None), pl.ds(0, rows))]
@@ -319,9 +338,9 @@
             gout[to] = acc[...].astype(jnp.bfloat16)
             put(b, to).start()
 
-        return n + last.astype(jnp.int32)
-
-    n = lax.fori_loop(0, total, step, jnp.int32(0))
+        return n + last.astype(jnp.int32), later
+
+    n, _ = lax.fori_loop(0, total, step, (jnp.int32(0), score(0)))
     for k in range(2):
         @pl.when(n > k)
         def _():
@@ -611,7 +630,7 @@
         value = (value + as_column(factor[i, :, 0:rows]) * wide) * factor_scale
         for k in range(nx):
             final[k, i] = value[:, k * depth:(k + 1) * depth]
-        for d in range(1, nx):
+        for d in sorted(range(1, nx), key=lambda d: abs(2 * d - nx)):
             end(d, i).start()
     whole = cluster[y, x]
     for k in range(len(pairs)):
@@ -685,7 +704,7 @@
         in_specs=[SMEM, SMEM, HBM, HBM, VMEM, HBM],
         out_specs=[VMEM, VMEM, HBM],
         input_output_aliases={5: 2},
-        scratch_shapes=[pltpu.SMEM((2, nw * ny + 8), jnp.int32)]
+        scratch_shapes=[pltpu.SMEM((nw * ny + 8,), jnp.int32)]
         + buffers_of(rows, width, nx, quarter)
         + [
             pltpu.VMEM((rows, width), jnp.float32),

time: 322 us -> 314 us (0.975)
  Pallas kernels: 305 us -> 298 us
    pallas_call x1, Pallas kernels: 20.5 us -> 9.2 us  [local(): flash_call(nw, ny, half, scale, rows, width, nx, quarter)]
    pallas_call x1, Pallas kernels: 96.8 us -> 100 us  [local(): return_call(sizes, scale, rows, width, per)]
where the time goes in v5:
time: 314 us; the launch traced here: 312 us
  Pallas kernels  298 us (95%)
  local copies, waits for them, and re-layouts  8.13 us (3%)
  other arithmetic  5.22 us (2%)
    pallas_call x1, Pallas kernels, local(): pl.pallas_call(functools.partial(gather_kernel, sizes), out_shape=(sds((n...  188 us
    pallas_call x1, Pallas kernels, local(): return_call(sizes, scale, rows, width, per)  100 us
    pallas_call x1, Pallas kernels, local(): flash_call(nw, ny, half, scale, rows, width, nx, quarter)  9.2 us

profile of v5, /device:TPU:1, one launch (start us, length us, event | category | flops | bytes accessed | tf_op | source)
XLA Modules:
  0.0 312.4 jit_solution(2130738189843167802)
XLA Ops:
  0.6 0.0 copy-start.2
  0.6 0.0 copy-start.1
  0.7 0.8 broadcast_in_dim_reshape.4
  1.5 0.7 fusion.1
  2.2 0.1 select_n.41
  2.3 0.1 select_reduce_fusion.1
  2.4 0.6 pad.4.codes
  3.0 3.5 %add_convert_fusion = bf16[32,64,512]{2,1,0:T(8,128)(2,1)} fusion(bf16[32,64,512]{2,1,0:T(8,128)(2,1)} %param.11, f32[32,512]{1,0:T(8,128)} %param.10), kind=kLoop, calls=%fused_computation | loop fusion | flops 3145728 | bytes 4259840 | tf_op jit(solution)/shard_map/convert_element_type | solution.py:775
  6.5 0.0 copy-done.2
  6.5 0.0 copy-done.1
  6.5 0.1 convert_reduce_fusion
  6.7 0.7 log_convert_fusion.shift
  7.4 188.2 %gather.1 = (bf16[4,4,2,16,64,512]{5,4,3,2,1,0:T(8,128)(2,1)}, bf16[16,2,400,512]{3,2,1,0:T(8,128)(2,1)}, bf16[4,32,256]{2,1,0:T(8,128)(2,1)}, bf16[64,192,512]{2,1,0:T(8,128)(2,1)}) custom-call(bf16[2,16,64,512]{3,2,1,0:T(8,128)(2,1)} %bitcast.18, bf16[1536,128]{1,0:T(8,128)(2,1)} %users.1, bf16[16,512]{1,0:T(8,128)(2,1)} %pad.4.codes, ...), custom_call_target="tpu_custom_call" | custom-call | tf_op jit(solution)/shard_map/gather/pallas_call | solution.py:793
  195.5 0.9 slice.9
  196.4 0.7 convolution_convert_fusion.codes
  197.1 0.0 copy-start
  197.1 9.2 %flash.1 = (f32[2,16,2,2,1,256]{5,4,3,2,1,0:T(1,128)}, f32[64,4,8,256]{3,2,1,0:T(8,128)}, bf16[64,192,512]{2,1,0:T(8,128)(2,1)}) custom-call(s32[64,4]{1,0:T(8,128)} %convolution_convert_fusion.codes, s32[1]{0:T(128)} %bitcast.4.mine, bf16[32,400,512]{2,1,0:T(8,128)(2,1)} %bitcast.15, ...), custom_call_target="tpu_custom_call", output_to_operand_aliasing={{2}: (5, {})} | custom-call | tf_op jit(solution)/shard_map/flash/pallas_call | solution.py:816
  206.3 0.0 copy-done
  206.4 0.1 squeeze.3
  206.5 0.1 add.86
  206.6 0.1 broadcast_in_dim.48
  206.7 0.7 broadcast_in_dim.49.names
  207.4 100.2 %return.1 = (f32[4,2,192,128]{3,2,1,0:T(8,128)}, f32[32,128]{1,0:T(8,128)}, f32[4,2,1,256]{3,2,1,0:T(1,128)}) custom-call(bf16[16,2,2,192,512]{4,3,2,1,0:T(8,128)(2,1)} %bitcast.17, f32[2,16,2,2,1,256]{5,4,3,2,1,0:T(1,128)} %get-tuple-element.18.stats, f32[64,4,8,256]{3,2,1,0:T(8,128)} %get-tuple-element.19.masses, s32[1,1024]{1,0:T(1,128)} %broadcast_in_dim.49.names, ...), custom_call_target="tpu_custom_call" | custom-call | tf_op jit(solution)/shard_map/return/pallas_call | solution.py:822
  307.6 0.7 slice_reduce_fusion
  308.3 0.7 reshape_squeeze.3
  309.0 2.1 copy.23
  311.1 1.3 copy.24
  (10 shorter events, 0.1 us)
Async XLA Ops:
  0.6 5.9 %copy-start.2 = (s32[32]{0:T(128)S(1)}, s32[32]{0:T(128)}, u32[]{:S(2)}) copy-start(s32[32]{0:T(128)} %param.14) | copy-start | bytes 388
  0.6 5.9 %copy-start.1 = (s32[32,256]{1,0:T(8,128)S(1)}, s32[32,256]{1,0:T(8,128)}, u32[]{:S(2)}) copy-start(s32[32,256]{1,0:T(8,128)} %param.15) | copy-start | bytes 98308
  197.1 9.2 %copy-start = (s32[64,4]{1,0:T(8,128)S(1)}, s32[64,4]{1,0:T(8,128)}, u32[]{:S(2)}) copy-start(s32[64,4]{1,0:T(8,128)} %convolution_convert_fusion.codes) | copy-start | bytes 3076

commit v6 on v5

--- a/solution.py
+++ b/solution.py
@@ -370,7 +370,7 @@
     user_grad, centroid_grad, losses,
     own, sib, long_out, long_in, short_out, short_in,
     klong_out, klong_in, kshort_out, kshort_in,
-    final, landed, parts, cluster, everyone, terms,
+    final, packed, landed, parts, cluster, everyone, terms,
     across, joined, came, mine, got, beside, lost, factor, positive,
     own_sem, sib_s, sib_r, long_s, long_r, short_s, short_r,
     kl_s, kl_r, ks_s, ks_r, fin_s, fin_r, cl_s, cl_r,
@@ -612,7 +612,7 @@
             tasks.pop(0)[1]()
     def end(d, i):
         px = lax.rem(x + d, nx)
-        return remote(final.at[px, i], landed.at[x, i], fin_s, fin_r, 2 * d + i, {"x": px})
+        return remote(packed.at[px, i], landed.at[x, i], fin_s, fin_r, 2 * d + i, {"x": px})
 
     ready(0)
     for i in range(2):
@@ -630,6 +630,7 @@
         value = (value + as_column(factor[i, :, 0:rows]) * wide) * factor_scale
         for k in range(nx):
             final[k, i] = value[:, k * depth:(k + 1) * depth]
+            packed[k, i] = final[k, i].astype(jnp.bfloat16)
         for d in sorted(range(1, nx), key=lambda d: abs(2 * d - nx)):
             end(d, i).start()
     whole = cluster[y, x]
@@ -647,7 +648,7 @@
             frm = lax.rem(x - d + nx, nx)
             landing = landed.at[frm, i]
             remote(landing, landing, fin_s, fin_r, 2 * d + i, {"x": frm}).wait_recv()
-            user_grad[pl.ds(frm, 1), i] = landed[pl.ds(frm, 1), i]
+            user_grad[pl.ds(frm, 1), i] = landed[pl.ds(frm, 1), i].astype(jnp.float32)
 
     for copy in crossing + [cluster_copy(k) for k in range(len(pairs))] + [over, beside_copy]:
         copy.wait_send()
@@ -732,7 +733,9 @@
             ring(nz), ring(nz), ring(steps), ring(steps), ring(steps - 1), ring(steps - 1),
             buffer(steps, 2, 1, lanes), buffer(steps, 2, 1, lanes),
             buffer(steps - 1, 2, 1, lanes), buffer(steps - 1, 2, 1, lanes),
-            buffer(nx, 2, rows, depth), buffer(nx, 2, rows, depth),
+            buffer(nx, 2, rows, depth),
+            pltpu.VMEM((nx, 2, rows, depth), jnp.bfloat16),
+            pltpu.VMEM((nx, 2, rows, depth), jnp.bfloat16),
             buffer(max(nx * ny - 1, 1), per, depth), buffer(ny, nx, per, depth),
             pltpu.VMEM((nw, 2 * rows, width), jnp.bfloat16),
             buffer(nw, ny * MASS_ROWS, width),

time: 314 us -> 311 us (level)
    pallas_call x1, Pallas kernels: 100 us -> 95.5 us  [local(): return_call(sizes, scale, rows, width, per)]
    pallas_call x1, Pallas kernels: 9.2 us -> 12.5 us  [local(): flash_call(nw, ny, half, scale, rows, width, nx, quarter)]
where the time goes in v6:
time: 311 us
  Pallas kernels  296 us (95%)
  local copies, waits for them, and re-layouts  8.13 us (3%)
  other arithmetic  5.22 us (2%)
    pallas_call x1, Pallas kernels, local(): pl.pallas_call(functools.partial(gather_kernel, sizes), out_shape=(sds((n...  188 us
    pallas_call x1, Pallas kernels, local(): return_call(sizes, scale, rows, width, per)  95.5 us
    pallas_call x1, Pallas kernels, local(): flash_call(nw, ny, half, scale, rows, width, nx, quarter)  12.5 us

profile of v6, /device:TPU:1, one launch (start us, length us, event | category | flops | bytes accessed | tf_op | source)
XLA Modules:
  0.0 311.0 jit_solution(14977796939698451271)
XLA Ops:
  0.6 0.0 copy-start.2
  0.6 0.0 copy-start.1
  0.7 0.8 broadcast_in_dim_reshape.4
  1.5 0.7 fusion.1
  2.2 0.1 select_n.41
  2.3 0.1 select_reduce_fusion.1
  2.4 0.6 pad.4.codes
  3.0 3.5 %add_convert_fusion = bf16[32,64,512]{2,1,0:T(8,128)(2,1)} fusion(bf16[32,64,512]{2,1,0:T(8,128)(2,1)} %param.11, f32[32,512]{1,0:T(8,128)} %param.10), kind=kLoop, calls=%fused_computation | loop fusion | flops 3145728 | bytes 4259840 | tf_op jit(solution)/shard_map/convert_element_type | solution.py:778
  6.5 0.0 copy-done.2
  6.5 0.0 copy-done.1
  6.5 0.1 convert_reduce_fusion
  6.7 0.7 log_convert_fusion.shift
  7.4 188.2 %gather.1 = (bf16[4,4,2,16,64,512]{5,4,3,2,1,0:T(8,128)(2,1)}, bf16[16,2,400,512]{3,2,1,0:T(8,128)(2,1)}, bf16[4,32,256]{2,1,0:T(8,128)(2,1)}, bf16[64,192,512]{2,1,0:T(8,128)(2,1)}) custom-call(bf16[2,16,64,512]{3,2,1,0:T(8,128)(2,1)} %bitcast.18, bf16[1536,128]{1,0:T(8,128)(2,1)} %users.1, bf16[16,512]{1,0:T(8,128)(2,1)} %pad.4.codes, ...), custom_call_target="tpu_custom_call" | custom-call | tf_op jit(solution)/shard_map/gather/pallas_call | solution.py:796
  195.5 0.9 slice.9
  196.4 0.7 convolution_convert_fusion.codes
  197.1 0.0 copy-start
  197.1 12.5 %flash.1 = (f32[2,16,2,2,1,256]{5,4,3,2,1,0:T(1,128)}, f32[64,4,8,256]{3,2,1,0:T(8,128)}, bf16[64,192,512]{2,1,0:T(8,128)(2,1)}) custom-call(s32[64,4]{1,0:T(8,128)} %convolution_convert_fusion.codes, s32[1]{0:T(128)} %bitcast.4.mine, bf16[32,400,512]{2,1,0:T(8,128)(2,1)} %bitcast.15, ...), custom_call_target="tpu_custom_call", output_to_operand_aliasing={{2}: (5, {})} | custom-call | tf_op jit(solution)/shard_map/flash/pallas_call | solution.py:819
  209.6 0.0 copy-done
  209.7 0.1 squeeze.3
  209.8 0.1 add.86
  209.9 0.1 broadcast_in_dim.48
  210.0 0.7 broadcast_in_dim.49.names
  210.7 95.5 %return.1 = (f32[4,2,192,128]{3,2,1,0:T(8,128)}, f32[32,128]{1,0:T(8,128)}, f32[4,2,1,256]{3,2,1,0:T(1,128)}) custom-call(bf16[16,2,2,192,512]{4,3,2,1,0:T(8,128)(2,1)} %bitcast.17, f32[2,16,2,2,1,256]{5,4,3,2,1,0:T(1,128)} %get-tuple-element.18.stats, f32[64,4,8,256]{3,2,1,0:T(8,128)} %get-tuple-element.19.masses, s32[1,1024]{1,0:T(1,128)} %broadcast_in_dim.49.names, ...), custom_call_target="tpu_custom_call" | custom-call | tf_op jit(solution)/shard_map/return/pallas_call | solution.py:825
  306.2 0.7 slice_reduce_fusion
  307.0 0.7 reshape_squeeze.3
  307.6 2.1 copy.23
  309.7 1.3 copy.24
  (10 shorter events, 0.1 us)
Async XLA Ops:
  0.6 5.9 %copy-start.2 = (s32[32]{0:T(128)S(1)}, s32[32]{0:T(128)}, u32[]{:S(2)}) copy-start(s32[32]{0:T(128)} %param.14) | copy-start | bytes 388
  0.6 5.9 %copy-start.1 = (s32[32,256]{1,0:T(8,128)S(1)}, s32[32,256]{1,0:T(8,128)}, u32[]{:S(2)}) copy-start(s32[32,256]{1,0:T(8,128)} %param.15) | copy-start | bytes 98308
  197.1 12.5 %copy-start = (s32[64,4]{1,0:T(8,128)S(1)}, s32[64,4]{1,0:T(8,128)}, u32[]{:S(2)}) copy-start(s32[64,4]{1,0:T(8,128)} %convolution_convert_fusion.codes) | copy-start | bytes 3076
